TPU v7x, 512 devices: a whole 4x8x8 slice. The times are simulated.
512 devices in a mesh: ctx: 32 (over y_lo, z, core), tp: 16 (over x, y_hi).
Axes of the slice: x: 4, y: 8 (y_hi: 4, y_lo: 2; y = y_hi * 2 + y_lo), z: 8, core: 2. Of those that a mesh axis runs over, the one named last changes fastest.
Arguments:
- projected: bfloat16 [3, 8192, 8192], P(None, 'ctx', 'tp'), may hold values from -6 to 6
- short_weight: float32 [3, 3, 8192], P(None, None, 'tp'), may hold values from -3.5 to 3.5
- filter_taps: float32 [8192, 8192], P(None, ('tp', 'ctx')), may hold values from -1.6 to 1.6, as said below
- out_weight: bfloat16 [8192, 8192], P('tp', 'ctx'), may hold values from -0.125 to 0.125
Outputs:
- block_out: bfloat16 [8192, 8192], P('ctx', 'tp')
Inputs may be any that keep to these rules, and one draw needn't show every extreme that they name: `filter_taps`: taps of each channel's causal filter.
All inputs are finite; a program needn't handle non-finite values.
Results may differ from a plain program's by a relative error of at most 0.017.
Values may be sent and summed in bfloat16 or wider, within the bound.
No kernel may reach another device: no remote copies, remote signals or barrier semaphores. Data moves between devices by JAX's collectives and lax.ppermute only.
A program may use at most 64 MiB of HBM per device.

v0:
```python
import math

import jax
import jax.numpy as jnp
from jax import lax
from jax.sharding import PartitionSpec as P


def short_filter(signal_in, tap_weights, lead_rows):
    row_count = signal_in.shape[1] - lead_rows
    total_sum = jnp.zeros((signal_in.shape[0], row_count, signal_in.shape[2]), jnp.float32)
    for offset in range(tap_weights.shape[1]):
        total_sum = (
            total_sum
            + tap_weights[:, offset][:, None, :]
            * signal_in[:, lead_rows - offset : lead_rows - offset + row_count, :]
        )
    return total_sum


def phase_table(row_count, col_count, period_len):
    product_idx = (
        jnp.arange(row_count, dtype=jnp.int32)[:, None]
        * jnp.arange(col_count, dtype=jnp.int32)[None, :]
        % period_len
    )
    angle_rad = product_idx.astype(jnp.float32) * (2.0 * math.pi / period_len)
    return (jnp.cos(angle_rad), jnp.sin(angle_rad))


def last_product(left_side, table):
    return jnp.matmul(left_side, table, precision=lax.Precision.HIGHEST)


def forward_spectrum(signal):
    half_rows = signal.shape[1]
    outer_rows = 2 * half_rows
    inner_width = signal.shape[2]
    cos_outer, sin_outer = phase_table(outer_rows, half_rows, outer_rows)
    real_part = jnp.einsum("kn,cnm->ckm", cos_outer, signal, precision=lax.Precision.HIGHEST)
    imag_part = -jnp.einsum("kn,cnm->ckm", sin_outer, signal, precision=lax.Precision.HIGHEST)
    cos_twist, sin_twist = phase_table(outer_rows, inner_width, outer_rows * inner_width)
    real_part, imag_part = (
        real_part * cos_twist + imag_part * sin_twist,
        imag_part * cos_twist - real_part * sin_twist,
    )
    cos_inner, sin_inner = phase_table(inner_width, inner_width, inner_width)
    out_real = last_product(real_part, cos_inner) + last_product(imag_part, sin_inner)
    out_imag = last_product(imag_part, cos_inner) - last_product(real_part, sin_inner)
    return (out_real, out_imag)


def inverse_signal(spec_real, spec_imag, half_rows):
    outer_rows = spec_real.shape[1]
    inner_width = spec_real.shape[2]
    cos_inner, sin_inner = phase_table(inner_width, inner_width, inner_width)
    mid_real = last_product(spec_real, cos_inner) - last_product(spec_imag, sin_inner)
    mid_imag = last_product(spec_imag, cos_inner) + last_product(spec_real, sin_inner)
    cos_twist, sin_twist = phase_table(outer_rows, inner_width, outer_rows * inner_width)
    mid_real, mid_imag = (
        mid_real * cos_twist - mid_imag * sin_twist,
        mid_imag * cos_twist + mid_real * sin_twist,
    )
    cos_outer, sin_outer = phase_table(half_rows, outer_rows, outer_rows)
    result = jnp.einsum("nk,ckm->cnm", cos_outer, mid_real, precision=lax.Precision.HIGHEST)
    result = result - jnp.einsum(
        "nk,ckm->cnm", sin_outer, mid_imag, precision=lax.Precision.HIGHEST
    )
    return result / (outer_rows * inner_width)


def long_filter(mixed_input, filter_taps):
    length_seq, channels = mixed_input.shape
    inner_width = 128
    half_rows = length_seq // inner_width
    signal = mixed_input.astype(jnp.float32).T.reshape(channels, half_rows, inner_width)
    kernel = filter_taps.T.reshape(channels, half_rows, inner_width)
    signal_real, signal_imag = forward_spectrum(signal)
    kernel_real, kernel_imag = forward_spectrum(kernel)
    spec_real = signal_real * kernel_real - signal_imag * kernel_imag
    spec_imag = signal_real * kernel_imag + signal_imag * kernel_real
    result = inverse_signal(spec_real, spec_imag, half_rows)
    return result.reshape(channels, length_seq).T


def shards(projected, short_weight, filter_taps, out_weight):
    channels = filter_taps.shape[1]
    lead_rows = short_weight.shape[1] - 1
    gathered = lax.all_to_all(projected, "ctx", split_axis=2, concat_axis=1, tiled=True)
    own_weight = lax.dynamic_slice_in_dim(
        short_weight, lax.axis_index("ctx") * channels, channels, 2
    )
    padded = jnp.pad(gathered.astype(jnp.float32), ((0, 0), (lead_rows, 0), (0, 0)))
    filtered = short_filter(padded, own_weight, lead_rows)
    mixed_input = (filtered[1] * filtered[2]).astype(jnp.bfloat16)
    long_output = lax.optimization_barrier(
        long_filter(mixed_input, filter_taps).astype(jnp.bfloat16)
    )
    sent_back = (filtered[0] * long_output.astype(jnp.float32)).astype(jnp.bfloat16)
    returned = lax.all_to_all(sent_back, "ctx", split_axis=0, concat_axis=1, tiled=True)
    full_weight = lax.all_gather(out_weight, "ctx", axis=1, tiled=True)
    partial_out = jnp.dot(returned, full_weight, preferred_element_type=jnp.float32)
    return lax.psum_scatter(partial_out.astype(jnp.bfloat16), "tp", scatter_dimension=1, tiled=True)


def solution(mesh):
    in_specs = (P(None, "ctx", "tp"), P(None, None, "tp"), P(None, ("tp", "ctx")), P("tp", "ctx"))
    out_specs = P("ctx", "tp")
    return jax.shard_map(shards, mesh=mesh, in_specs=in_specs, out_specs=out_specs, check_vma=False)
```

profile of v0, /device:TPU:1, one launch (start us, length us, event | category | flops | bytes accessed | tf_op | source)
XLA Modules:
  0.0 241.3 jit_solution(8958893077133538602)
XLA Ops:
  6.5 0.7 all-gather.2.cloned.1.call-update
  7.3 2.4 copy.46
  9.7 13.0 %all-to-all-start = ((bf16[3,256,512]{1,0,2:T(4,128)(2,1)}), bf16[3,256,512]{1,0,2:T(4,128)(2,1)}, u32[]{:S(2)}, u32[]{:S(2)}) async-start(bf16[3,256,512]{1,0,2:T(4,128)(2,1)} %copy.46), calls=%async_computation | async-start | bytes 2097152 | tf_op jit(solution)/shard_map/all_to_all | solution.py:89
  22.9 0.3 fusion.82
  23.2 1.2 convolution_negate_fusion
  24.3 1.2 fusion.61
  25.5 0.9 constant_dynamic-slice_fusion.1
  26.6 1.2 fusion.7
  27.8 1.2 fusion.3
  29.1 1.2 convolution_add_fusion.1
  30.3 2.2 convolution_subtract_fusion.1
  32.5 20.4 %all-to-all-done = bf16[3,256,512]{1,0,2:T(4,128)(2,1)} async-done(((bf16[3,256,512]{1,0,2:T(4,128)(2,1)}), bf16[3,256,512]{1,0,2:T(4,128)(2,1)}, u32[]{:S(2)}, u32[]{:S(2)}) %all-to-all-start) | async-done | bytes 786464 | tf_op jit(solution)/shard_map/all_to_all | solution.py:89
  53.0 1.3 copy.47
  54.3 0.2 convert_bitcast_fusion
  54.7 0.9 multiply_add_fusion
  55.7 0.7 convolution_bitcast_fusion
  56.4 0.7 fusion
  57.2 2.2 fusion.24
  59.4 2.0 fusion.23
  61.4 2.0 convolution_add_fusion.2
  63.5 2.2 multiply_subtract_fusion
  65.7 1.3 fusion.38
  67.0 1.3 fusion.36
  68.3 1.3 convolution_subtract_fusion
  69.7 1.3 convolution_add_fusion
  71.0 1.7 fusion.12
  72.7 1.5 fusion.2
  74.2 0.2 copy.85
  74.5 17.4 %all_to_all.28 = bf16[32,256,16]{1,2,0:T(8,128)(2,1)S(1)} all-to-all(bf16[32,256,16]{1,2,0:T(8,128)(2,1)S(1)} %bitcast.119), channel_id=1, replica_groups=mesh['ctx'=32,'tp'=16] {'ctx'}, dimensions={0} | all-to-all | bytes 524288 | tf_op jit(solution)/shard_map/all_to_all | solution.py:100
  91.9 37.2 %all-gather.2.cloned.1.call-done = bf16[512,8192]{1,0:T(8,128)(2,1)} async-done(((bf16[512,256]{1,0:T(8,128)(2,1)}), bf16[512,8192]{1,0:T(8,128)(2,1)}) %all-gather.2.cloned.1.call-update) | async-done | bytes 8388624 | tf_op jit(solution)/shard_map/all_gather | solution.py:101
  129.1 7.7 %convolution_convert_fusion = bf16[256,8192]{1,0:T(8,128)(2,1)} fusion(bf16[256,512]{0,1:T(8,128)(2,1)S(1)} %bitcast.118, bf16[512,8192]{1,0:T(8,128)(2,1)} %all-gather.2.cloned.1.call-done), kind=kOutput, calls=%fused_computation | convolution fusion | flops 2149580800 | bytes 12845056 | tf_op jit(solution)/shard_map/dot_general | solution.py:102
  136.8 97.6 %reduce-scatter.2.cloned.1.call-done = bf16[256,512]{1,0:T(8,128)(2,1)} async-done(((bf16[256,8192]{1,0:T(8,128)(2,1)}), bf16[256,512]{1,0:T(8,128)(2,1)}) %reduce-scatter.2.cloned.1.call-update) | async-done | bytes 262160 | tf_op jit(solution)/shard_map/reduce_scatter | solution.py:103
  (17 shorter events, 0.7 us)
Async XLA Ops:
  6.5 122.6 %all-gather.2.cloned.1.call-start = ((), (), s32[]{:S(2)}) async-start(), calls=%async_computation.3 | async-start | bytes 8650752 | tf_op jit(solution)/shard_map/all_gather | solution.py:101
  7.3 15.5 %copy-start.1 = (f32[8192,16]{0,1:T(8,128)S(1)}, f32[8192,16]{0,1:T(8,128)}, u32[]{:S(2)}) copy-start(f32[8192,16]{0,1:T(8,128)} %param.6) | copy-start | bytes 1572868
  9.7 43.3 %all-to-all-start = ((bf16[3,256,512]{1,0,2:T(4,128)(2,1)}), bf16[3,256,512]{1,0,2:T(4,128)(2,1)}, u32[]{:S(2)}, u32[]{:S(2)}) async-start(bf16[3,256,512]{1,0,2:T(4,128)(2,1)} %copy.46), calls=%async_computation | async-start | bytes 2097152 | tf_op jit(solution)/shard_map/all_to_all | solution.py:89
  22.7 211.8 %reduce-scatter.2.cloned.1.call-start = ((), (), s32[]{:S(2)}) async-start(), calls=%async_computation.4 | async-start | bytes 4456448 | tf_op jit(solution)/shard_map/reduce_scatter | solution.py:103
  61.4 2.1 copy-start
Sparse Core Ops, SparseCore 0:
  9.4 119.6 all-gather.1
  137.0 97.4 reduce-scatter.1
where the time goes:
time: 242 us; the launch traced here: 241 us
  waiting for transfers between devices  156 us (64%)
  matrix products  34.4 us (14%)
  blocking collectives  17.4 us (7%)
  between operations  13.6 us (6%)
  starting transfers between devices  13.1 us (5%)
  local copies, waits for them, and re-layouts  5.29 us (2%)
    reduce_scatter x1, waiting for transfers between devices, shards(): lax.psum_scatter(partial_out.astype(jnp.bfloat16), 'tp', scatter_dimensio...  97.6 us
    all_gather x1, waiting for transfers between devices, shards(): full_weight = lax.all_gather(out_weight, 'ctx', axis=1, tiled=True)  37.2 us
    all_to_all x1, waiting for transfers between devices, shards(): lax.all_to_all(projected, 'ctx', split_axis=2, concat_axis=1, tiled=True)  20.4 us
    dot_general x12, matrix products, last_product(): return jnp.matmul(left_side, table, precision=lax.Precision.HIGHEST)  19.7 us
    all_to_all x1, blocking collectives, shards(): lax.all_to_all(sent_back, 'ctx', split_axis=0, concat_axis=1, tiled=True)  17.4 us
    all_to_all x1, starting transfers between devices, shards(): lax.all_to_all(projected, 'ctx', split_axis=2, concat_axis=1, tiled=True)  13 us
    dot_general x1, matrix products, shards(): jnp.dot(returned, full_weight, preferred_element_type=jnp.float32)  7.72 us
  transfers between devices with their start and end apart: 3, of which 3 were waited for; matrix products, arithmetic and copies ran while one was open for 14% of the time, Pallas kernels for 0%

commit v1 on v0

v1 whole, which is shorter than its diff:
```python
import functools

import jax
import jax.numpy as jnp
import ml_dtypes
import numpy as np
from jax import lax
from jax.experimental import pallas as pl
from jax.experimental.pallas import tpu as pltpu
from jax.sharding import Mesh, PartitionSpec as P

F32, BF16 = jnp.float32, jnp.bfloat16
CTX = ("yl", "z", "c")
BLOCKS = 32
CH = 16
WIDE = 256
TOKENS = BLOCKS * WIDE
MIB = 1024 * 1024
VMEM = pl.BlockSpec(memory_space=pltpu.VMEM)
ANY = pl.BlockSpec(memory_space=pl.ANY)
SMEM = pl.BlockSpec(memory_space=pltpu.SMEM)


def call(kernel, out_shape, n_scalar, n_in, scratch=(), n_dep=0, vmem=56, flops=1000):
    return pl.pallas_call(
        kernel,
        out_shape=out_shape,
        in_specs=[ANY] * n_dep + [SMEM] * n_scalar + [VMEM] * n_in,
        out_specs=jax.tree.map(lambda _: VMEM, out_shape),
        scratch_shapes=list(scratch),
        compiler_params=pltpu.CompilerParams(vmem_limit_bytes=vmem * MIB),
        cost_estimate=pl.CostEstimate(flops=flops, bytes_accessed=1000, transcendentals=0),
    )


def table16(table):
    return table.astype(ml_dtypes.bfloat16)


@functools.lru_cache(None)
def tables():
    turn = 2.0 * np.pi
    eye = np.eye(CH)
    k1 = np.arange(BLOCKS) + 0.25
    n1 = np.arange(BLOCKS)
    outer = turn * np.outer(k1, n1) / BLOCKS
    first = np.concatenate([np.cos(outer), -np.sin(outer)], 0)
    first = np.kron(first, eye)
    last = np.concatenate([np.cos(outer.T), -np.sin(outer.T)], 1) / TOKENS
    last = np.kron(last, eye)
    n2 = np.arange(WIDE)
    twist = (turn * np.outer(k1, n2) / TOKENS)[:, None, :]
    inner = turn * (np.outer(n2, n2) % WIDE) / WIDE
    c, s = np.cos(inner), np.sin(inner)
    forward = np.block([[c, -s], [s, c]])
    backward = np.block([[c, s], [-s, c]])
    return dict(
        first=table16(first),
        last=table16(last),
        forward=table16(forward),
        backward=table16(backward),
        twist=(np.cos(twist).astype(np.float32), np.sin(twist).astype(np.float32)),
    )


def dot(a, b):
    return jnp.dot(a, b, preferred_element_type=F32)


def turn(re, im, cos, sin):
    shape = (BLOCKS, CH, WIDE)
    re, im = re.reshape(shape), im.reshape(shape)
    flat = (BLOCKS * CH, WIDE)
    return (re * cos + im * sin).reshape(flat), (im * cos - re * sin).reshape(flat)


def featurize_kernel(projected, lead, weight, mixed, query, padded):
    def filtered(m):
        padded[0:8, :] = jnp.zeros((8, padded.shape[1]), F32)
        padded[6:8, :] = lead[m].astype(F32)
        padded[8:, :] = projected[m].astype(F32)
        rows = projected.shape[1]
        total = weight[m, 0:1, :] * padded[8 : 8 + rows, :]
        total = total + weight[m, 1:2, :] * padded[7 : 7 + rows, :]
        return total + weight[m, 2:3, :] * padded[6 : 6 + rows, :]

    product = filtered(1) * filtered(2)
    mixed[...] = product.T.astype(BF16).reshape(mixed.shape)
    query[...] = filtered(0).T


def filter_kernel(taps, first, cos, sin, fwd, spectrum):
    rows = BLOCKS * CH
    outer = dot(first[...], taps[...].reshape(rows, WIDE).astype(BF16))
    turned = turn(outer[:rows], outer[rows:], cos[...], sin[...])
    spectrum[...] = dot(jnp.concatenate(turned, 1).astype(BF16), fwd[...])


def conv_kernel(dep, signal, spectrum, first, cos, sin, fwd, bwd, last, out):
    del dep
    rows = BLOCKS * CH
    outer = dot(first[...], signal[...].reshape(rows, WIDE))
    turned = turn(outer[:rows], outer[rows:], cos[...], sin[...])
    spec = dot(jnp.concatenate(turned, 1).astype(BF16), fwd[...])
    sr, si = spec[:, :WIDE], spec[:, WIDE:]
    hr, hi = spectrum[:, :WIDE], spectrum[:, WIDE:]
    both = jnp.concatenate([sr * hr - si * hi, sr * hi + si * hr], 1).astype(BF16)
    mid = dot(both, bwd[...])
    turned = turn(mid[:, :WIDE], mid[:, WIDE:], cos[...], -sin[...])
    out[...] = dot(last[...], jnp.concatenate(turned, 0).astype(BF16)).astype(BF16).reshape(out.shape)


def gate_kernel(dep, convolved, query, gated):
    del dep
    rows = (query[...] * convolved[...].reshape(query.shape).astype(F32)).T.astype(BF16)
    for copy in range(gated.shape[0]):
        gated[copy] = rows


def pair_kernel(signal, spectrum, own, mate, out):
    del signal, spectrum
    out[0] = own[...]
    out[1] = mate[...]


def quad_kernel(dep, own, other, out):
    del dep
    out[:, :, :WIDE] = own[...]
    out[:, :, WIDE:] = other[...]


def project_kernel(place, g_own, g_other, w0, w1, w2, w3, w4, keep, send, total):
    yl, z, core = place[0], place[1], place[2]
    total[...] = jnp.zeros_like(total)

    def add(step, row, block):
        source = (z + 8 + step * (2 * core - 1)) % 8
        group = 2 * row + source // 4
        total[group, 0] += dot(g_own[source % 4], block)
        total[group, 1] += dot(g_other[source % 4], block)

    mine = lax.rem(yl + core, 2)
    add(0, mine, w0[core])
    for step, ref in ((1, w1), (2, w2), (3, w3)):
        add(step, yl, ref[0])
        add(step, 1 - yl, ref[1])
    add(4, mine, w4[...])

    own = pl.ds(pl.multiple_of(core * WIDE, WIDE), WIDE)
    other = pl.ds(pl.multiple_of((1 - core) * WIDE, WIDE), WIDE)
    for group in range(4):
        for tokens, ref in ((0, keep), (1, send)):
            ref[group, :, own] = total[group, tokens, :, :WIDE].astype(BF16)
            ref[group, :, other] = total[group, tokens, :, WIDE:].astype(BF16)


def ring(n, shift):
    return [(i, (i + shift) % n) for i in range(n)]


def swap_pairs():
    def index(h, w, yh):
        return (4 * h + w) * 4 + yh

    return [(index(h, w, yh), index(h, yh, w)) for h in range(2) for w in range(4) for yh in range(4)]


def along(a):
    pairs = [((z * 2 + c), ((z + 1 - 2 * c) % 8) * 2 + c) for z in range(8) for c in range(2)]
    return lax.ppermute(a, ("z", "c"), pairs)


def tie(dep, *arrays, flops=1000):
    n = len(arrays)
    return pl.pallas_call(
        lambda *refs: None,
        out_shape=[jax.ShapeDtypeStruct(a.shape, a.dtype) for a in arrays],
        in_specs=[ANY] * (n + 1),
        out_specs=[ANY] * n,
        input_output_aliases={i + 1: i for i in range(n)},
        cost_estimate=pl.CostEstimate(flops=flops, bytes_accessed=1000, transcendentals=0),
    )(dep, *arrays)


def shards(projected, short_weight, filter_taps, out_weight):
    t = tables()
    width = projected.shape[2]
    rows = projected.shape[1]
    core = lax.axis_index("c")
    place = jnp.stack([lax.axis_index("yl"), lax.axis_index("z"), core]).astype(jnp.int32)

    order = [(i, i + 1) for i in range(BLOCKS - 1)]
    lead = lax.ppermute(projected[:, -2:], CTX, order)
    block = lax.ppermute(out_weight, ("z", "yh"), swap_pairs())

    mixed, query = call(
        featurize_kernel,
        [jax.ShapeDtypeStruct((BLOCKS, CH, WIDE), BF16), jax.ShapeDtypeStruct((width, rows), F32)],
        0, 3,
        [pltpu.VMEM((rows + 8, width), F32)],
    )(projected, lead, short_weight)
    signal = lax.all_to_all(mixed, CTX, split_axis=0, concat_axis=0, tiled=True)

    taps = filter_taps.T.reshape(CH, BLOCKS, WIDE).transpose(1, 0, 2)
    taps, = tie(mixed, taps)
    block, = tie(mixed, block)
    mate = lax.ppermute(block, "yl", ring(2, 1))
    spectrum = call(
        filter_kernel, jax.ShapeDtypeStruct((BLOCKS * CH, 2 * WIDE), F32), 0, 5
    )(taps, t["first"], *t["twist"], t["forward"])

    pair = call(pair_kernel, jax.ShapeDtypeStruct((2, width, WIDE), BF16), 0, 2, n_dep=2)(
        signal, spectrum, block, mate
    )
    other = lax.ppermute(pair, "c", ring(2, 1))
    convolved = call(
        conv_kernel, jax.ShapeDtypeStruct((BLOCKS, CH, WIDE), BF16), 0, 8, n_dep=1
    )(pair, signal, spectrum, t["first"], *t["twist"], t["forward"], t["backward"], t["last"])
    w0 = call(quad_kernel, jax.ShapeDtypeStruct((2, width, 2 * WIDE), BF16), 0, 2, n_dep=1)(
        convolved, pair, other
    )
    w1 = along(w0)
    convolved, = tie(w0, convolved)
    convolved = lax.all_to_all(convolved, CTX, split_axis=0, concat_axis=0, tiled=True)

    w1, = tie(convolved, w1)
    w2 = along(w1)
    gated = call(
        gate_kernel, jax.ShapeDtypeStruct((4, rows, width), BF16), 0, 2, n_dep=1
    )(w1, convolved, query)
    w2, = tie(gated, w2)
    w3 = along(w2)
    half = lax.dynamic_index_in_dim(w3, core, 0, keepdims=False)
    w4, = tie(half, along(half), flops=10**9)

    g_own = lax.all_to_all(gated, "yh", split_axis=0, concat_axis=0, tiled=True)
    g_own, = tie(half, g_own)
    g_other = lax.ppermute(g_own, "c", ring(2, 1))

    keep, send = call(
        project_kernel,
        [jax.ShapeDtypeStruct((4, rows, width), BF16)] * 2,
        1, 7,
        [pltpu.VMEM((4, 2, rows, width), F32)],
        vmem=24,
    )(place, g_own, g_other, w0, w1, w2, w3, w4)
    partial = (keep.astype(F32) + lax.ppermute(send, "c", ring(2, 1)).astype(F32)).astype(BF16)
    parts = lax.all_to_all(partial, "x", split_axis=0, concat_axis=0, tiled=True)
    return jnp.sum(parts.astype(F32), 0).astype(BF16)


def solution(mesh):
    fine = Mesh(mesh.devices.reshape(2, 8, 2, 4, 4), ("yl", "z", "c", "x", "yh"))
    tp = ("x", "yh")
    in_specs = (P(None, CTX, tp), P(None, None, tp), P(None, tp + CTX), P(tp, CTX))
    out_specs = P(CTX, tp)
    return jax.shard_map(shards, mesh=fine, in_specs=in_specs, out_specs=out_specs, check_vma=False)
```

time: 242 us -> 169 us (0.70)
  waiting for transfers between devices: 156 us -> 34.3 us
  starting transfers between devices: 13.1 us -> 60.4 us
  matrix products: 34.4 us -> 0 us
  Pallas kernels: 0 us -> 21.9 us
  blocking collectives: 17.4 us -> 37.7 us
  between operations: 13.6 us -> 0.19 us
  local copies, waits for them, and re-layouts: 5.29 us -> 11.4 us
    reduce_scatter x1 -> x0, waiting for transfers between devices: 97.6 us -> none  [shards(): lax.psum_scatter(partial_out.astype(jnp.bfloat16), 'tp', scatter_dimensio...]
    ppermute x0 -> x10, starting transfers between devices: none -> 42 us  [the longest x4 17.2 us: along(): return lax.ppermute(a, ('z', 'c'), pairs)]
    all_gather x1 -> x0, waiting for transfers between devices: 37.2 us -> none  [shards(): full_weight = lax.all_gather(out_weight, 'ctx', axis=1, tiled=True)]
    dot_general x19 -> x0, matrix products: 34.4 us -> none  [the longest x12 19.7 us: last_product(): return jnp.matmul(left_side, table, precision=lax.Precision.HIGHEST)]
    ppermute x0 -> x10, waiting for transfers between devices: none -> 31.9 us  [the longest x4 28.2 us: along(): return lax.ppermute(a, ('z', 'c'), pairs)]
    pallas_call x0 -> x14, Pallas kernels: none -> 21.9 us  [the longest x1 4.89 us: shards(): call(conv_kernel, jax.ShapeDtypeStruct((BLOCKS, CH, WIDE), BF16), 0, 8, n...]
    all_to_all x1 -> x2, blocking collectives: 17.4 us -> 37.7 us  [the longest x1 19.7 us: shards(): lax.all_to_all(convolved, CTX, split_axis=0, concat_axis=0, tiled=True)]
    all_to_all x1 -> x2, waiting for transfers between devices: 20.4 us -> 2.35 us  [the longest x1 2.35 us: shards(): signal = lax.all_to_all(mixed, CTX, split_axis=0, concat_axis=0, tiled=True)]
  transfers between devices with their start and end apart: 3 -> 12, of which waited for: 3 -> 6; matrix products, arithmetic and copies ran while one was open for 14% -> 2% of each run, Pallas kernels for 0% -> 8%
where the time goes in v1:
time: 169 us; the launch traced here: 167 us
  starting transfers between devices  60.4 us (36%)
  blocking collectives  37.7 us (22%)
  waiting for transfers between devices  34.3 us (20%)
  Pallas kernels  21.9 us (13%)
  local copies, waits for them, and re-layouts  11.4 us (7%)
    ppermute x4, waiting for transfers between devices, along(): return lax.ppermute(a, ('z', 'c'), pairs)  28.2 us
    all_to_all x1, blocking collectives, shards(): lax.all_to_all(convolved, CTX, split_axis=0, concat_axis=0, tiled=True)  19.7 us
    all_to_all x1, blocking collectives, shards(): lax.all_to_all(partial, 'x', split_axis=0, concat_axis=0, tiled=True)  18 us
    ppermute x4, starting transfers between devices, along(): return lax.ppermute(a, ('z', 'c'), pairs)  17.2 us
    all_to_all x1, starting transfers between devices, shards(): signal = lax.all_to_all(mixed, CTX, split_axis=0, concat_axis=0, tiled=True)  14.8 us
    unnamed x30, local copies, waits for them, and re-layouts  8.91 us
    ppermute x1, starting transfers between devices, shards(): lead = lax.ppermute(projected[:, -2:], CTX, order)  7.51 us
    ppermute x1, starting transfers between devices, shards(): g_other = lax.ppermute(g_own, 'c', ring(2, 1))  6.42 us
  transfers between devices with their start and end apart: 12, of which 6 were waited for; matrix products, arithmetic and copies ran while one was open for 2% of the time, Pallas kernels for 8%

profile of v1, /device:TPU:1, one launch (start us, length us, event | category | flops | bytes accessed | tf_op | source)
XLA Modules:
  0.0 167.1 jit_solution(13932911018828509329)
XLA Ops:
  0.0 1.6 collective-permute-start.1
  2.4 7.5 %collective-permute-start = (bf16[3,2,512]{2,1,0:T(2,128)(2,1)S(1)}, bf16[3,2,512]{2,1,0:T(2,128)(2,1)S(1)}, u32[]{:S(2)}, u32[]{:S(2)}) collective-permute-start(bf16[3,2,512]{2,1,0:T(2,128)(2,1)S(1)} %slice.3), channel_id=1, source_target_pairs={{0,16},{16,32},{32,48},{48,64},{64,80},{80,96},{96,112},{112,128},... | collective-permute-start | bytes 18440 | tf_op jit(solution)/shard_map/ppermute | solution.py:193
  9.9 1.4 collective-permute-done.lead
  11.9 2.6 %shard_map.100 = (bf16[32,16,256]{2,1,0:T(8,128)(2,1)}, f32[512,256]{1,0:T(8,128)}) custom-call(bf16[3,256,512]{2,1,0:T(8,128)(2,1)} %projected.1, bf16[3,2,512]{2,1,0:T(2,128)(2,1)} %copy-done.14, f32[3,3,512]{2,1,0:T(4,128)} %weight.1), custom_call_target="tpu_custom_call" | custom-call | flops 1000 | bytes 1000 | tf_op jit(solution)/shard_map/pallas_call | solution.py:196
  14.5 14.8 %all-to-all-start = ((bf16[32,16,256]{2,1,0:T(8,128)(2,1)}), bf16[32,16,256]{2,1,0:T(8,128)(2,1)S(1)}, u32[]{:S(2)}, u32[]{:S(2)}) async-start(bf16[32,16,256]{2,1,0:T(8,128)(2,1)} %get-tuple-element.9.refs_0_), calls=%async_computation | async-start | bytes 524288 | tf_op jit(solution)/shard_map/all_to_all | solution.py:202
  30.1 3.3 %collective-permute-start.2 = (bf16[512,256]{1,0:T(8,128)(2,1)}, bf16[512,256]{1,0:T(8,128)(2,1)S(1)}, u32[]{:S(2)}, u32[]{:S(2)}) collective-permute-start(bf16[512,256]{1,0:T(8,128)(2,1)} %shard_map.103.own), channel_id=1, source_target_pairs={{0,256},{256,0},{1,257},{257,1},{2,258},{258,2},{3,259},{259,3},{4... | collective-permute-start | bytes 786440 | tf_op jit(solution)/shard_map/ppermute | solution.py:207
  34.2 3.8 %shard_map.102.spectrum = f32[512,512]{1,0:T(8,128)} custom-call(f32[32,16,256]{2,1,0:T(8,128)} %shard_map.101.taps, bf16[1024,512]{1,0:T(8,128)(2,1)} %constant.37.clone.first, f32[32,1,256]{2,1,0:T(1,128)} %constant.38.clone.cos, f32[32,1,256]{2,1,0:T(1,128)} %constant.39.clone.sin, bf16[512,512]{1,0:T(8,128)(2,1)} %constant.40.clone.fwd), custom_call_target="tpu_custom_call" | custom-call | flops 1000 | bytes 1000 | tf_op jit(solution)/shard_map/pallas_call | solution.py:208
  38.0 2.3 %all-to-all-done.signal = bf16[32,16,256]{2,1,0:T(8,128)(2,1)S(1)} async-done(((bf16[32,16,256]{2,1,0:T(8,128)(2,1)}), bf16[32,16,256]{2,1,0:T(8,128)(2,1)S(1)}, u32[]{:S(2)}, u32[]{:S(2)}) %all-to-all-start) | async-done | bytes 262176 | tf_op jit(solution)/shard_map/all_to_all | solution.py:202
  41.8 1.9 %shard_map.104.dep.own = bf16[2,512,256]{2,1,0:T(8,128)(2,1)} custom-call(bf16[32,16,256]{2,1,0:T(8,128)(2,1)} %copy-done.9, f32[512,512]{1,0:T(8,128)} %shard_map.102.spectrum, bf16[512,256]{1,0:T(8,128)(2,1)} %shard_map.103.own, bf16[512,256]{1,0:T(8,128)(2,1)} %copy-done.13), custom_call_target="tpu_custom_call" | custom-call | flops 1000 | bytes 1000 | tf_op jit(solution)/shard_map/pallas_call | solution.py:212
  43.6 1.9 %collective-permute-start.3 = (bf16[2,512,256]{2,1,0:T(8,128)(2,1)}, bf16[2,512,256]{2,1,0:T(8,128)(2,1)S(1)}, u32[]{:S(2)}, u32[]{:S(2)}) collective-permute-start(bf16[2,512,256]{2,1,0:T(8,128)(2,1)} %shard_map.104.dep.own), channel_id=1, source_target_pairs={{0,16},{16,0},{1,17},{17,1},{2,18},{18,2},{3,19},{19,3},{4,20},{20... | collective-permute-start | bytes 1572872 | tf_op jit(solution)/shard_map/ppermute | solution.py:215
  45.5 4.9 %shard_map.105.dep.refs_1_ = bf16[32,16,256]{2,1,0:T(8,128)(2,1)} custom-call(bf16[2,512,256]{2,1,0:T(8,128)(2,1)} %shard_map.104.dep.own, bf16[32,16,256]{2,1,0:T(8,128)(2,1)} %copy-done.9, f32[512,512]{1,0:T(8,128)} %shard_map.102.spectrum, bf16[1024,512]{1,0:T(8,128)(2,1)} %constant.37.clone.first, f32[32,1,256]{2,1,0:T(1,128)} %constant.38.clone.cos, ...), custom_call_target="tpu_custom_call" | custom-call | flops 1000 | bytes 1000 | tf_op jit(solution)/shard_map/pallas_call | solution.py:216
  51.2 2.3 %shard_map.106.refs_0_.w0 = bf16[2,512,512]{2,1,0:T(8,128)(2,1)} custom-call(bf16[32,16,256]{2,1,0:T(8,128)(2,1)} %shard_map.105.dep.refs_1_, bf16[2,512,256]{2,1,0:T(8,128)(2,1)} %shard_map.104.dep.own, bf16[2,512,256]{2,1,0:T(8,128)(2,1)} %copy-done.12), custom_call_target="tpu_custom_call" | custom-call | flops 1000 | bytes 1000 | tf_op jit(solution)/shard_map/pallas_call | solution.py:219
  53.5 8.9 %collective-permute-start.4 = (bf16[2,512,512]{2,1,0:T(8,128)(2,1)}, bf16[2,512,512]{2,1,0:T(8,128)(2,1)S(1)}, u32[]{:S(2)}, u32[]{:S(2)}) collective-permute-start(bf16[2,512,512]{2,1,0:T(8,128)(2,1)} %shard_map.106.refs_0_.w0), channel_id=1, source_target_pairs={{0,32},{16,240},{32,64},{48,16},{64,96},{80,48},{96,128},{112,80},... | collective-permute-start | bytes 3145736 | tf_op jit(solution)/shard_map/ppermute | solution.py:170
  62.4 19.7 %all_to_all.20.refs_0_.convolved = bf16[32,16,256]{2,1,0:T(8,128)(2,1)} all-to-all(bf16[32,16,256]{2,1,0:T(8,128)(2,1)} %shard_map.107), channel_id=1, replica_groups=mesh['yl'=2,'z'=8,'c'=2,'x'=4,'yh'=4] {'yl','z','c'}, dimensions={0} | all-to-all | bytes 524288 | tf_op jit(solution)/shard_map/all_to_all | solution.py:224
  82.1 1.0 copy-done.3
  83.1 2.6 %collective-permute-start.5 = (bf16[2,512,512]{2,1,0:T(8,128)(2,1)}, bf16[2,512,512]{2,1,0:T(8,128)(2,1)S(1)}, u32[]{:S(2)}, u32[]{:S(2)}) collective-permute-start(bf16[2,512,512]{2,1,0:T(8,128)(2,1)} %shard_map.108.dep.w1), channel_id=1, source_target_pairs={{0,32},{16,240},{32,64},{48,16},{64,96},{80,48},{96,128},{112,80},... | collective-permute-start | bytes 3145736 | tf_op jit(solution)/shard_map/ppermute | solution.py:170
  85.7 2.3 %shard_map.109.refs_0_ = bf16[4,256,512]{2,1,0:T(8,128)(2,1)} custom-call(bf16[2,512,512]{2,1,0:T(8,128)(2,1)} %shard_map.108.dep.w1, bf16[32,16,256]{2,1,0:T(8,128)(2,1)} %all_to_all.20.refs_0_.convolved, f32[512,256]{1,0:T(8,128)} %get-tuple-element.10.query), custom_call_target="tpu_custom_call" | custom-call | flops 1000 | bytes 1000 | tf_op jit(solution)/shard_map/pallas_call | solution.py:228
  88.0 3.6 %all-to-all-start.2 = ((bf16[4,256,512]{2,1,0:T(8,128)(2,1)}), bf16[4,256,512]{2,1,0:T(8,128)(2,1)S(1)}, u32[]{:S(2)}, u32[]{:S(2)}) async-start(bf16[4,256,512]{2,1,0:T(8,128)(2,1)} %shard_map.109.refs_0_), calls=%async_computation.2 | async-start | bytes 2097152 | tf_op jit(solution)/shard_map/all_to_all | solution.py:236
  91.6 7.5 %collective-permute-done.5.refs_1_ = bf16[2,512,512]{2,1,0:T(8,128)(2,1)S(1)} collective-permute-done((bf16[2,512,512]{2,1,0:T(8,128)(2,1)}, bf16[2,512,512]{2,1,0:T(8,128)(2,1)S(1)}, u32[]{:S(2)}, u32[]{:S(2)}) %collective-permute-start.5) | collective-permute-done | bytes 1048608 | tf_op jit(solution)/shard_map/ppermute | solution.py:170
  99.1 1.0 copy-done.5
  100.1 3.8 %collective-permute-start.6 = (bf16[2,512,512]{2,1,0:T(8,128)(2,1)}, bf16[2,512,512]{2,1,0:T(8,128)(2,1)S(1)}, u32[]{:S(2)}, u32[]{:S(2)}) collective-permute-start(bf16[2,512,512]{2,1,0:T(8,128)(2,1)} %shard_map.110.w2), channel_id=1, source_target_pairs={{0,32},{16,240},{32,64},{48,16},{64,96},{80,48},{96,128},{112,80},... | collective-permute-start | bytes 3145736 | tf_op jit(solution)/shard_map/ppermute | solution.py:170
  104.0 12.2 %collective-permute-done.6.w3 = bf16[2,512,512]{2,1,0:T(8,128)(2,1)S(1)} collective-permute-done((bf16[2,512,512]{2,1,0:T(8,128)(2,1)}, bf16[2,512,512]{2,1,0:T(8,128)(2,1)S(1)}, u32[]{:S(2)}, u32[]{:S(2)}) %collective-permute-start.6) | collective-permute-done | bytes 1048608 | tf_op jit(solution)/shard_map/ppermute | solution.py:170
  117.1 1.0 copy-done.1
  118.1 6.4 %collective-permute-start.7 = (bf16[4,256,512]{2,1,0:T(8,128)(2,1)}, bf16[4,256,512]{2,1,0:T(8,128)(2,1)}, u32[]{:S(2)}, u32[]{:S(2)}) collective-permute-start(bf16[4,256,512]{2,1,0:T(8,128)(2,1)} %shard_map.111.g_own), channel_id=1, source_target_pairs={{0,16},{16,0},{1,17},{17,1},{2,18},{18,2},{3,19},{19,3},{4,20},{20... | collective-permute-start | bytes 3145736 | tf_op jit(solution)/shard_map/ppermute | solution.py:238
  124.5 1.9 %collective-permute-start.8 = (bf16[512,512]{1,0:T(8,128)(2,1)}, bf16[512,512]{1,0:T(8,128)(2,1)}, u32[]{:S(2)}, u32[]{:S(2)}) collective-permute-start(bf16[512,512]{1,0:T(8,128)(2,1)} %dynamic-slice_bitcast_fusion.refs_0_), channel_id=1, source_target_pairs={{0,32},{16,240},{32,64},{48,16},{64,96},{80,48},{96,128},{112,80},... | collective-permute-start | bytes 1572872 | tf_op jit(solution)/shard_map/ppermute | solution.py:170
  126.5 8.5 %collective-permute-done.8.refs_1_ = bf16[512,512]{1,0:T(8,128)(2,1)} collective-permute-done((bf16[512,512]{1,0:T(8,128)(2,1)}, bf16[512,512]{1,0:T(8,128)(2,1)}, u32[]{:S(2)}, u32[]{:S(2)}) %collective-permute-start.8) | collective-permute-done | bytes 524320 | tf_op jit(solution)/shard_map/ppermute | solution.py:170
  135.1 1.2 copy-done.6
  136.3 1.2 copy-done.8
  137.5 4.1 %shard_map.113 = (bf16[4,256,512]{2,1,0:T(8,128)(2,1)S(1)}, bf16[4,256,512]{2,1,0:T(8,128)(2,1)S(1)}) custom-call(s32[3]{0:T(128)S(1)} %pad_add_fusion.place, bf16[4,256,512]{2,1,0:T(8,128)(2,1)S(1)} %copy-done.2, bf16[4,256,512]{2,1,0:T(8,128)(2,1)} %collective-permute-done.7.g_other, bf16[2,512,512]{2,1,0:T(8,128)(2,1)S(1)} %copy-done, ...), custom_call_target="tpu_custom_call" | custom-call | flops 1000 | bytes 1000 | tf_op jit(solution)/shard_map/pallas_call | solution.py:240
  141.6 4.0 %collective-permute-start.9 = (bf16[4,256,512]{2,1,0:T(8,128)(2,1)S(1)}, bf16[4,256,512]{2,1,0:T(8,128)(2,1)S(1)}, u32[]{:S(2)}, u32[]{:S(2)}) collective-permute-start(bf16[4,256,512]{2,1,0:T(8,128)(2,1)S(1)} %get-tuple-element.12), channel_id=1, source_target_pairs={{0,16},{16,0},{1,17},{17,1},{2,18},{18,2},{3,19},{19,3},{4,20},{20... | collective-permute-start | bytes 3145736 | tf_op jit(solution)/shard_map/ppermute | solution.py:247
  145.6 2.3 %collective-permute-done.9 = bf16[4,256,512]{2,1,0:T(8,128)(2,1)S(1)} collective-permute-done((bf16[4,256,512]{2,1,0:T(8,128)(2,1)S(1)}, bf16[4,256,512]{2,1,0:T(8,128)(2,1)S(1)}, u32[]{:S(2)}, u32[]{:S(2)}) %collective-permute-start.9) | collective-permute-done | bytes 1048608 | tf_op jit(solution)/shard_map/ppermute | solution.py:247
  148.2 18.0 %all_to_all.21 = bf16[4,256,512]{2,1,0:T(8,128)(2,1)S(1)} all-to-all(bf16[4,256,512]{2,1,0:T(8,128)(2,1)S(1)} %add_convert_fusion), channel_id=1, replica_groups=mesh['yl'=2,'z'=8,'c'=2,'x'=4,'yh'=4] {'x'}, dimensions={0} | all-to-all | bytes 2097152 | tf_op jit(solution)/shard_map/all_to_all | solution.py:248
  (44 shorter events, 7.3 us)
Async XLA Ops:
  0.0 29.4 %collective-permute-start.1 = (bf16[512,256]{1,0:T(8,128)(2,1)}, bf16[512,256]{1,0:T(8,128)(2,1)S(1)}, u32[]{:S(2)}, u32[]{:S(2)}) collective-permute-start(bf16[512,256]{1,0:T(8,128)(2,1)} %param.13), channel_id=1, source_target_pairs={{0,0},{1,32},{2,64},{3,96},{32,1},{33,33},{34,65},{35,97},{64,2},{... | collective-permute-start | bytes 786440 | tf_op jit(solution)/shard_map/ppermute | solution.py:194
  2.3 31.0 %copy-start.11 = (f32[8192,16]{0,1:T(8,128)S(1)}, f32[8192,16]{0,1:T(8,128)}, u32[]{:S(2)}) copy-start(f32[8192,16]{0,1:T(8,128)} %param.12) | copy-start | bytes 1572868
  2.4 8.9 %collective-permute-start = (bf16[3,2,512]{2,1,0:T(2,128)(2,1)S(1)}, bf16[3,2,512]{2,1,0:T(2,128)(2,1)S(1)}, u32[]{:S(2)}, u32[]{:S(2)}) collective-permute-start(bf16[3,2,512]{2,1,0:T(2,128)(2,1)S(1)} %slice.3), channel_id=1, source_target_pairs={{0,16},{16,32},{32,48},{48,64},{64,80},{80,96},{96,112},{112,128},... | collective-permute-start | bytes 18440 | tf_op jit(solution)/shard_map/ppermute | solution.py:193
  11.3 0.6 copy-start.14
  14.5 25.8 %all-to-all-start = ((bf16[32,16,256]{2,1,0:T(8,128)(2,1)}), bf16[32,16,256]{2,1,0:T(8,128)(2,1)S(1)}, u32[]{:S(2)}, u32[]{:S(2)}) async-start(bf16[32,16,256]{2,1,0:T(8,128)(2,1)} %get-tuple-element.9.refs_0_), calls=%async_computation | async-start | bytes 524288 | tf_op jit(solution)/shard_map/all_to_all | solution.py:202
  29.4 0.7 copy-start.10
  30.1 10.3 %collective-permute-start.2 = (bf16[512,256]{1,0:T(8,128)(2,1)}, bf16[512,256]{1,0:T(8,128)(2,1)S(1)}, u32[]{:S(2)}, u32[]{:S(2)}) collective-permute-start(bf16[512,256]{1,0:T(8,128)(2,1)} %shard_map.103.own), channel_id=1, source_target_pairs={{0,256},{256,0},{1,257},{257,1},{2,258},{258,2},{3,259},{259,3},{4... | collective-permute-start | bytes 786440 | tf_op jit(solution)/shard_map/ppermute | solution.py:207
  40.4 0.7 copy-start.9
  41.1 0.7 copy-start.13
  43.6 6.8 %collective-permute-start.3 = (bf16[2,512,256]{2,1,0:T(8,128)(2,1)}, bf16[2,512,256]{2,1,0:T(8,128)(2,1)S(1)}, u32[]{:S(2)}, u32[]{:S(2)}) collective-permute-start(bf16[2,512,256]{2,1,0:T(8,128)(2,1)} %shard_map.104.dep.own), channel_id=1, source_target_pairs={{0,16},{16,0},{1,17},{17,1},{2,18},{18,2},{3,19},{19,3},{4,20},{20... | collective-permute-start | bytes 1572872 | tf_op jit(solution)/shard_map/ppermute | solution.py:215
  50.4 0.8 copy-start.12
  53.5 28.6 %collective-permute-start.4 = (bf16[2,512,512]{2,1,0:T(8,128)(2,1)}, bf16[2,512,512]{2,1,0:T(8,128)(2,1)S(1)}, u32[]{:S(2)}, u32[]{:S(2)}) collective-permute-start(bf16[2,512,512]{2,1,0:T(8,128)(2,1)} %shard_map.106.refs_0_.w0), channel_id=1, source_target_pairs={{0,32},{16,240},{32,64},{48,16},{64,96},{80,48},{96,128},{112,80},... | collective-permute-start | bytes 3145736 | tf_op jit(solution)/shard_map/ppermute | solution.py:170
  82.1 1.0 copy-start.3
  83.1 16.0 %collective-permute-start.5 = (bf16[2,512,512]{2,1,0:T(8,128)(2,1)}, bf16[2,512,512]{2,1,0:T(8,128)(2,1)S(1)}, u32[]{:S(2)}, u32[]{:S(2)}) collective-permute-start(bf16[2,512,512]{2,1,0:T(8,128)(2,1)} %shard_map.108.dep.w1), channel_id=1, source_target_pairs={{0,32},{16,240},{32,64},{48,16},{64,96},{80,48},{96,128},{112,80},... | collective-permute-start | bytes 3145736 | tf_op jit(solution)/shard_map/ppermute | solution.py:170
  88.0 29.1 %all-to-all-start.2 = ((bf16[4,256,512]{2,1,0:T(8,128)(2,1)}), bf16[4,256,512]{2,1,0:T(8,128)(2,1)S(1)}, u32[]{:S(2)}, u32[]{:S(2)}) async-start(bf16[4,256,512]{2,1,0:T(8,128)(2,1)} %shard_map.109.refs_0_), calls=%async_computation.2 | async-start | bytes 2097152 | tf_op jit(solution)/shard_map/all_to_all | solution.py:236
  99.1 1.0 copy-start.5
  100.1 16.0 %collective-permute-start.6 = (bf16[2,512,512]{2,1,0:T(8,128)(2,1)}, bf16[2,512,512]{2,1,0:T(8,128)(2,1)S(1)}, u32[]{:S(2)}, u32[]{:S(2)}) collective-permute-start(bf16[2,512,512]{2,1,0:T(8,128)(2,1)} %shard_map.110.w2), channel_id=1, source_target_pairs={{0,32},{16,240},{32,64},{48,16},{64,96},{80,48},{96,128},{112,80},... | collective-permute-start | bytes 3145736 | tf_op jit(solution)/shard_map/ppermute | solution.py:170
  116.2 1.9 %copy-start.7 = (bf16[2,512,512]{2,1,0:T(8,128)(2,1)}, bf16[2,512,512]{2,1,0:T(8,128)(2,1)S(1)}, u32[]{:S(2)}) copy-start(bf16[2,512,512]{2,1,0:T(8,128)(2,1)S(1)} %collective-permute-done.6.w3) | copy-start | bytes 3145732
  117.1 1.0 copy-start.1
  118.1 17.0 %collective-permute-start.7 = (bf16[4,256,512]{2,1,0:T(8,128)(2,1)}, bf16[4,256,512]{2,1,0:T(8,128)(2,1)}, u32[]{:S(2)}, u32[]{:S(2)}) collective-permute-start(bf16[4,256,512]{2,1,0:T(8,128)(2,1)} %shard_map.111.g_own), channel_id=1, source_target_pairs={{0,16},{16,0},{1,17},{17,1},{2,18},{18,2},{3,19},{19,3},{4,20},{20... | collective-permute-start | bytes 3145736 | tf_op jit(solution)/shard_map/ppermute | solution.py:238
  124.5 10.5 %collective-permute-start.8 = (bf16[512,512]{1,0:T(8,128)(2,1)}, bf16[512,512]{1,0:T(8,128)(2,1)}, u32[]{:S(2)}, u32[]{:S(2)}) collective-permute-start(bf16[512,512]{1,0:T(8,128)(2,1)} %dynamic-slice_bitcast_fusion.refs_0_), channel_id=1, source_target_pairs={{0,32},{16,240},{32,64},{48,16},{64,96},{80,48},{96,128},{112,80},... | collective-permute-start | bytes 1572872 | tf_op jit(solution)/shard_map/ppermute | solution.py:170
  126.5 8.5 %copy-start = (bf16[2,512,512]{2,1,0:T(8,128)(2,1)S(1)}, bf16[2,512,512]{2,1,0:T(8,128)(2,1)}, u32[]{:S(2)}) copy-start(bf16[2,512,512]{2,1,0:T(8,128)(2,1)} %shard_map.106.refs_0_.w0) | copy-start | bytes 3145732
  126.5 8.5 %copy-start.2 = (bf16[4,256,512]{2,1,0:T(8,128)(2,1)S(1)}, bf16[4,256,512]{2,1,0:T(8,128)(2,1)}, u32[]{:S(2)}) copy-start(bf16[4,256,512]{2,1,0:T(8,128)(2,1)} %shard_map.111.g_own) | copy-start | bytes 3145732
  126.5 8.5 %copy-start.4 = (bf16[2,512,512]{2,1,0:T(8,128)(2,1)S(1)}, bf16[2,512,512]{2,1,0:T(8,128)(2,1)}, u32[]{:S(2)}) copy-start(bf16[2,512,512]{2,1,0:T(8,128)(2,1)} %shard_map.108.dep.w1) | copy-start | bytes 3145732
  135.1 1.2 copy-start.6
  136.3 1.2 copy-start.8
  141.6 6.3 %collective-permute-start.9 = (bf16[4,256,512]{2,1,0:T(8,128)(2,1)S(1)}, bf16[4,256,512]{2,1,0:T(8,128)(2,1)S(1)}, u32[]{:S(2)}, u32[]{:S(2)}) collective-permute-start(bf16[4,256,512]{2,1,0:T(8,128)(2,1)S(1)} %get-tuple-element.12), channel_id=1, source_target_pairs={{0,16},{16,0},{1,17},{17,1},{2,18},{18,2},{3,19},{19,3},{4,20},{20... | collective-permute-start | bytes 3145736 | tf_op jit(solution)/shard_map/ppermute | solution.py:247

commit v2 on v1

--- a/solution.py
+++ b/solution.py
@@ -110,8 +110,7 @@
     out[...] = dot(last[...], jnp.concatenate(turned, 0).astype(BF16)).astype(BF16).reshape(out.shape)
 
 
-def gate_kernel(dep, convolved, query, gated):
-    del dep
+def gate_kernel(convolved, query, gated):
     rows = (query[...] * convolved[...].reshape(query.shape).astype(F32)).T.astype(BF16)
     for copy in range(gated.shape[0]):
         gated[copy] = rows
@@ -221,20 +220,19 @@
     )
     w1 = along(w0)
     convolved, = tie(w0, convolved)
+    w1, = tie(convolved, w1)
     convolved = lax.all_to_all(convolved, CTX, split_axis=0, concat_axis=0, tiled=True)
-
-    w1, = tie(convolved, w1)
     w2 = along(w1)
     gated = call(
-        gate_kernel, jax.ShapeDtypeStruct((4, rows, width), BF16), 0, 2, n_dep=1
-    )(w1, convolved, query)
+        gate_kernel, jax.ShapeDtypeStruct((4, rows, width), BF16), 0, 2, flops=6 * 10**9
+    )(convolved, query)
     w2, = tie(gated, w2)
     w3 = along(w2)
     half = lax.dynamic_index_in_dim(w3, core, 0, keepdims=False)
-    w4, = tie(half, along(half), flops=10**9)
+    w4, = tie(half, along(half), flops=10**10)
 
     g_own = lax.all_to_all(gated, "yh", split_axis=0, concat_axis=0, tiled=True)
-    g_own, = tie(half, g_own)
+    g_own, = tie(half, g_own, flops=10**10)
     g_other = lax.ppermute(g_own, "c", ring(2, 1))
 
     keep, send = call(

time: 169 us -> 163 us (0.964)
  blocking collectives: 37.7 us -> 18 us
  starting transfers between devices: 60.4 us -> 68.7 us
  waiting for transfers between devices: 34.3 us -> 39.8 us
    all_to_all x1 -> x0, blocking collectives: 19.7 us -> none  [shards(): lax.all_to_all(convolved, CTX, split_axis=0, concat_axis=0, tiled=True)]
    ppermute x4, starting transfers between devices: 17.2 us -> 23.9 us  [along(): return lax.ppermute(a, ('z', 'c'), pairs)]
    ppermute x4, waiting for transfers between devices: 28.2 us -> 33.7 us  [along(): return lax.ppermute(a, ('z', 'c'), pairs)]
    ppermute x1, starting transfers between devices: 6.42 us -> 1.91 us  [shards(): g_other = lax.ppermute(g_own, 'c', ring(2, 1))]
    all_to_all x0 -> x1, starting transfers between devices: none -> 4.36 us  [shards(): lax.all_to_all(convolved, CTX, split_axis=0, concat_axis=0, tiled=True)]
    ppermute x1, starting transfers between devices: 3.99 us -> 5.87 us  [shards(): lax.ppermute(send, 'c', ring(2, 1)).astype(F32)]
    unnamed x30 -> x32, local copies, waits for them, and re-layouts: 8.91 us -> 9.63 us
  transfers between devices with their start and end apart: 12 -> 13, of which waited for: 6 -> 7; matrix products, arithmetic and copies ran while one was open for 2% -> 2% of each run, Pallas kernels for 8% -> 8%
where the time goes in v2:
time: 163 us; the launch traced here: 162 us
  starting transfers between devices  68.7 us (42%)
  waiting for transfers between devices  39.8 us (24%)
  Pallas kernels  21.8 us (13%)
  blocking collectives  18 us (11%)
  local copies, waits for them, and re-layouts  12.2 us (7%)
    ppermute x4, waiting for transfers between devices, along(): return lax.ppermute(a, ('z', 'c'), pairs)  33.7 us
    ppermute x4, starting transfers between devices, along(): return lax.ppermute(a, ('z', 'c'), pairs)  23.9 us
    all_to_all x1, blocking collectives, shards(): lax.all_to_all(partial, 'x', split_axis=0, concat_axis=0, tiled=True)  18 us
    all_to_all x1, starting transfers between devices, shards(): signal = lax.all_to_all(mixed, CTX, split_axis=0, concat_axis=0, tiled=True)  14.8 us
    unnamed x32, local copies, waits for them, and re-layouts  9.63 us
    ppermute x1, starting transfers between devices, shards(): lead = lax.ppermute(projected[:, -2:], CTX, order)  7.51 us
    ppermute x1, starting transfers between devices, shards(): lax.ppermute(send, 'c', ring(2, 1)).astype(F32)  5.87 us
    pallas_call x1, Pallas kernels, shards(): call(conv_kernel, jax.ShapeDtypeStruct((BLOCKS, CH, WIDE), BF16), 0, 8, n...  4.87 us
  transfers between devices with their start and end apart: 13, of which 7 were waited for; matrix products, arithmetic and copies ran while one was open for 2% of the time, Pallas kernels for 8%

profile of v2, /device:TPU:1, one launch (start us, length us, event | category | flops | bytes accessed | tf_op | source)
XLA Modules:
  0.0 162.0 jit_solution(15403481614516174361)
XLA Ops:
  0.0 1.6 collective-permute-start.1
  2.4 7.5 %collective-permute-start = (bf16[3,2,512]{2,1,0:T(2,128)(2,1)S(1)}, bf16[3,2,512]{2,1,0:T(2,128)(2,1)S(1)}, u32[]{:S(2)}, u32[]{:S(2)}) collective-permute-start(bf16[3,2,512]{2,1,0:T(2,128)(2,1)S(1)} %slice.3), channel_id=1, source_target_pairs={{0,16},{16,32},{32,48},{48,64},{64,80},{80,96},{96,112},{112,128},... | collective-permute-start | bytes 18440 | tf_op jit(solution)/shard_map/ppermute | solution.py:192
  9.9 1.4 collective-permute-done.lead
  11.9 2.7 %shard_map.100 = (bf16[32,16,256]{2,1,0:T(8,128)(2,1)}, f32[512,256]{1,0:T(8,128)}) custom-call(bf16[3,256,512]{2,1,0:T(8,128)(2,1)} %projected.1, bf16[3,2,512]{2,1,0:T(2,128)(2,1)} %copy-done.15, f32[3,3,512]{2,1,0:T(4,128)} %weight.1), custom_call_target="tpu_custom_call" | custom-call | flops 1000 | bytes 1000 | tf_op jit(solution)/shard_map/pallas_call | solution.py:195
  14.6 14.8 %all-to-all-start = ((bf16[32,16,256]{2,1,0:T(8,128)(2,1)}), bf16[32,16,256]{2,1,0:T(8,128)(2,1)S(1)}, u32[]{:S(2)}, u32[]{:S(2)}) async-start(bf16[32,16,256]{2,1,0:T(8,128)(2,1)} %get-tuple-element.9.refs_0_), calls=%async_computation | async-start | bytes 524288 | tf_op jit(solution)/shard_map/all_to_all | solution.py:201
  30.1 3.3 %collective-permute-start.2 = (bf16[512,256]{1,0:T(8,128)(2,1)}, bf16[512,256]{1,0:T(8,128)(2,1)S(1)}, u32[]{:S(2)}, u32[]{:S(2)}) collective-permute-start(bf16[512,256]{1,0:T(8,128)(2,1)} %shard_map.103.own), channel_id=1, source_target_pairs={{0,256},{256,0},{1,257},{257,1},{2,258},{258,2},{3,259},{259,3},{4... | collective-permute-start | bytes 786440 | tf_op jit(solution)/shard_map/ppermute | solution.py:206
  34.3 3.8 %shard_map.102.spectrum = f32[512,512]{1,0:T(8,128)} custom-call(f32[32,16,256]{2,1,0:T(8,128)} %shard_map.101.taps, bf16[1024,512]{1,0:T(8,128)(2,1)} %constant.37.clone.first, f32[32,1,256]{2,1,0:T(1,128)} %constant.38.clone.cos, f32[32,1,256]{2,1,0:T(1,128)} %constant.39.clone.sin, bf16[512,512]{1,0:T(8,128)(2,1)} %constant.40.clone.fwd), custom_call_target="tpu_custom_call" | custom-call | flops 1000 | bytes 1000 | tf_op jit(solution)/shard_map/pallas_call | solution.py:207
  38.0 2.4 %all-to-all-done.signal = bf16[32,16,256]{2,1,0:T(8,128)(2,1)S(1)} async-done(((bf16[32,16,256]{2,1,0:T(8,128)(2,1)}), bf16[32,16,256]{2,1,0:T(8,128)(2,1)S(1)}, u32[]{:S(2)}, u32[]{:S(2)}) %all-to-all-start) | async-done | bytes 262176 | tf_op jit(solution)/shard_map/all_to_all | solution.py:201
  41.8 1.9 %shard_map.104.dep.own = bf16[2,512,256]{2,1,0:T(8,128)(2,1)} custom-call(bf16[32,16,256]{2,1,0:T(8,128)(2,1)} %copy-done.9, f32[512,512]{1,0:T(8,128)} %shard_map.102.spectrum, bf16[512,256]{1,0:T(8,128)(2,1)} %shard_map.103.own, bf16[512,256]{1,0:T(8,128)(2,1)} %copy-done.13), custom_call_target="tpu_custom_call" | custom-call | flops 1000 | bytes 1000 | tf_op jit(solution)/shard_map/pallas_call | solution.py:211
  43.7 1.9 %collective-permute-start.3 = (bf16[2,512,256]{2,1,0:T(8,128)(2,1)}, bf16[2,512,256]{2,1,0:T(8,128)(2,1)S(1)}, u32[]{:S(2)}, u32[]{:S(2)}) collective-permute-start(bf16[2,512,256]{2,1,0:T(8,128)(2,1)} %shard_map.104.dep.own), channel_id=1, source_target_pairs={{0,16},{16,0},{1,17},{17,1},{2,18},{18,2},{3,19},{19,3},{4,20},{20... | collective-permute-start | bytes 1572872 | tf_op jit(solution)/shard_map/ppermute | solution.py:214
  45.6 4.9 %shard_map.105.dep.refs_1_ = bf16[32,16,256]{2,1,0:T(8,128)(2,1)} custom-call(bf16[2,512,256]{2,1,0:T(8,128)(2,1)} %shard_map.104.dep.own, bf16[32,16,256]{2,1,0:T(8,128)(2,1)} %copy-done.9, f32[512,512]{1,0:T(8,128)} %shard_map.102.spectrum, bf16[1024,512]{1,0:T(8,128)(2,1)} %constant.37.clone.first, f32[32,1,256]{2,1,0:T(1,128)} %constant.38.clone.cos, ...), custom_call_target="tpu_custom_call" | custom-call | flops 1000 | bytes 1000 | tf_op jit(solution)/shard_map/pallas_call | solution.py:215
  51.3 2.3 %shard_map.106.refs_0_.w0 = bf16[2,512,512]{2,1,0:T(8,128)(2,1)} custom-call(bf16[32,16,256]{2,1,0:T(8,128)(2,1)} %shard_map.105.dep.refs_1_, bf16[2,512,256]{2,1,0:T(8,128)(2,1)} %shard_map.104.dep.own, bf16[2,512,256]{2,1,0:T(8,128)(2,1)} %copy-done.12), custom_call_target="tpu_custom_call" | custom-call | flops 1000 | bytes 1000 | tf_op jit(solution)/shard_map/pallas_call | solution.py:218
  53.5 8.9 %collective-permute-start.4 = (bf16[2,512,512]{2,1,0:T(8,128)(2,1)}, bf16[2,512,512]{2,1,0:T(8,128)(2,1)S(1)}, u32[]{:S(2)}, u32[]{:S(2)}) collective-permute-start(bf16[2,512,512]{2,1,0:T(8,128)(2,1)} %shard_map.106.refs_0_.w0), channel_id=1, source_target_pairs={{0,32},{16,240},{32,64},{48,16},{64,96},{80,48},{96,128},{112,80},... | collective-permute-start | bytes 3145736 | tf_op jit(solution)/shard_map/ppermute | solution.py:169
  62.4 4.4 %all-to-all-start.1 = ((bf16[32,16,256]{2,1,0:T(8,128)(2,1)}), bf16[32,16,256]{2,1,0:T(8,128)(2,1)S(1)}, u32[]{:S(2)}, u32[]{:S(2)}) async-start(bf16[32,16,256]{2,1,0:T(8,128)(2,1)} %shard_map.107.refs_0_), calls=%async_computation.1 | async-start | bytes 524288 | tf_op jit(solution)/shard_map/all_to_all | solution.py:224
  66.8 12.7 %collective-permute-done.4.refs_1_ = bf16[2,512,512]{2,1,0:T(8,128)(2,1)S(1)} collective-permute-done((bf16[2,512,512]{2,1,0:T(8,128)(2,1)}, bf16[2,512,512]{2,1,0:T(8,128)(2,1)S(1)}, u32[]{:S(2)}, u32[]{:S(2)}) %collective-permute-start.4) | collective-permute-done | bytes 1048608 | tf_op jit(solution)/shard_map/ppermute | solution.py:169
  80.5 4.9 %collective-permute-start.5 = (bf16[2,512,512]{2,1,0:T(8,128)(2,1)}, bf16[2,512,512]{2,1,0:T(8,128)(2,1)S(1)}, u32[]{:S(2)}, u32[]{:S(2)}) collective-permute-start(bf16[2,512,512]{2,1,0:T(8,128)(2,1)} %shard_map.109.w1), channel_id=1, source_target_pairs={{0,32},{16,240},{32,64},{48,16},{64,96},{80,48},{96,128},{112,80},... | collective-permute-start | bytes 3145736 | tf_op jit(solution)/shard_map/ppermute | solution.py:169
  86.1 2.3 %shard_map.108.refs_0_ = bf16[4,256,512]{2,1,0:T(8,128)(2,1)} custom-call(bf16[32,16,256]{2,1,0:T(8,128)(2,1)} %copy-done.14, f32[512,256]{1,0:T(8,128)} %get-tuple-element.10.query), custom_call_target="tpu_custom_call" | custom-call | flops 6000000000 | bytes 1000 | tf_op jit(solution)/shard_map/pallas_call | solution.py:226
  88.4 3.5 %all-to-all-start.2 = ((bf16[4,256,512]{2,1,0:T(8,128)(2,1)}), bf16[4,256,512]{2,1,0:T(8,128)(2,1)S(1)}, u32[]{:S(2)}, u32[]{:S(2)}) async-start(bf16[4,256,512]{2,1,0:T(8,128)(2,1)} %shard_map.108.refs_0_), calls=%async_computation.2 | async-start | bytes 2097152 | tf_op jit(solution)/shard_map/all_to_all | solution.py:234
  91.9 5.5 %collective-permute-done.5.refs_1_ = bf16[2,512,512]{2,1,0:T(8,128)(2,1)S(1)} collective-permute-done((bf16[2,512,512]{2,1,0:T(8,128)(2,1)}, bf16[2,512,512]{2,1,0:T(8,128)(2,1)S(1)}, u32[]{:S(2)}, u32[]{:S(2)}) %collective-permute-start.5) | collective-permute-done | bytes 1048608 | tf_op jit(solution)/shard_map/ppermute | solution.py:169
  97.4 1.0 copy-done.1
  98.5 5.2 %collective-permute-start.6 = (bf16[2,512,512]{2,1,0:T(8,128)(2,1)}, bf16[2,512,512]{2,1,0:T(8,128)(2,1)S(1)}, u32[]{:S(2)}, u32[]{:S(2)}) collective-permute-start(bf16[2,512,512]{2,1,0:T(8,128)(2,1)} %shard_map.110.w2), channel_id=1, source_target_pairs={{0,32},{16,240},{32,64},{48,16},{64,96},{80,48},{96,128},{112,80},... | collective-permute-start | bytes 3145736 | tf_op jit(solution)/shard_map/ppermute | solution.py:169
  103.7 12.0 %collective-permute-done.6.w3 = bf16[2,512,512]{2,1,0:T(8,128)(2,1)S(1)} collective-permute-done((bf16[2,512,512]{2,1,0:T(8,128)(2,1)}, bf16[2,512,512]{2,1,0:T(8,128)(2,1)S(1)}, u32[]{:S(2)}, u32[]{:S(2)}) %collective-permute-start.6) | collective-permute-done | bytes 1048608 | tf_op jit(solution)/shard_map/ppermute | solution.py:169
  116.6 4.9 %collective-permute-start.8 = (bf16[512,512]{1,0:T(8,128)(2,1)}, bf16[512,512]{1,0:T(8,128)(2,1)}, u32[]{:S(2)}, u32[]{:S(2)}) collective-permute-start(bf16[512,512]{1,0:T(8,128)(2,1)} %dynamic-slice_bitcast_fusion.refs_0_), channel_id=1, source_target_pairs={{0,32},{16,240},{32,64},{48,16},{64,96},{80,48},{96,128},{112,80},... | collective-permute-start | bytes 1572872 | tf_op jit(solution)/shard_map/ppermute | solution.py:169
  121.6 1.0 copy-done.3
  122.6 1.9 %collective-permute-start.7 = (bf16[4,256,512]{2,1,0:T(8,128)(2,1)}, bf16[4,256,512]{2,1,0:T(8,128)(2,1)}, u32[]{:S(2)}, u32[]{:S(2)}) collective-permute-start(bf16[4,256,512]{2,1,0:T(8,128)(2,1)} %shard_map.111.g_own), channel_id=1, source_target_pairs={{0,16},{16,0},{1,17},{17,1},{2,18},{18,2},{3,19},{19,3},{4,20},{20... | collective-permute-start | bytes 3145736 | tf_op jit(solution)/shard_map/ppermute | solution.py:236
  124.6 3.4 %collective-permute-done.8.refs_1_ = bf16[512,512]{1,0:T(8,128)(2,1)} collective-permute-done((bf16[512,512]{1,0:T(8,128)(2,1)}, bf16[512,512]{1,0:T(8,128)(2,1)}, u32[]{:S(2)}, u32[]{:S(2)}) %collective-permute-start.8) | collective-permute-done | bytes 524320 | tf_op jit(solution)/shard_map/ppermute | solution.py:169
  128.0 1.2 copy-done.6
  129.2 1.2 copy-done.8
  130.4 4.1 %shard_map.113 = (bf16[4,256,512]{2,1,0:T(8,128)(2,1)S(1)}, bf16[4,256,512]{2,1,0:T(8,128)(2,1)S(1)}) custom-call(s32[3]{0:T(128)S(1)} %pad_add_fusion.place, bf16[4,256,512]{2,1,0:T(8,128)(2,1)S(1)} %copy-done.4, bf16[4,256,512]{2,1,0:T(8,128)(2,1)} %collective-permute-done.7.g_other, bf16[2,512,512]{2,1,0:T(8,128)(2,1)S(1)} %copy-done, ...), custom_call_target="tpu_custom_call" | custom-call | flops 1000 | bytes 1000 | tf_op jit(solution)/shard_map/pallas_call | solution.py:238
  134.6 5.9 %collective-permute-start.9 = (bf16[4,256,512]{2,1,0:T(8,128)(2,1)S(1)}, bf16[4,256,512]{2,1,0:T(8,128)(2,1)S(1)}, u32[]{:S(2)}, u32[]{:S(2)}) collective-permute-start(bf16[4,256,512]{2,1,0:T(8,128)(2,1)S(1)} %get-tuple-element.12), channel_id=1, source_target_pairs={{0,16},{16,0},{1,17},{17,1},{2,18},{18,2},{3,19},{19,3},{4,20},{20... | collective-permute-start | bytes 3145736 | tf_op jit(solution)/shard_map/ppermute | solution.py:245
  140.5 2.3 %collective-permute-done.9 = bf16[4,256,512]{2,1,0:T(8,128)(2,1)S(1)} collective-permute-done((bf16[4,256,512]{2,1,0:T(8,128)(2,1)S(1)}, bf16[4,256,512]{2,1,0:T(8,128)(2,1)S(1)}, u32[]{:S(2)}, u32[]{:S(2)}) %collective-permute-start.9) | collective-permute-done | bytes 1048608 | tf_op jit(solution)/shard_map/ppermute | solution.py:245
  143.0 18.0 %all_to_all.20 = bf16[4,256,512]{2,1,0:T(8,128)(2,1)S(1)} all-to-all(bf16[4,256,512]{2,1,0:T(8,128)(2,1)S(1)} %add_convert_fusion), channel_id=1, replica_groups=mesh['yl'=2,'z'=8,'c'=2,'x'=4,'yh'=4] {'x'}, dimensions={0} | all-to-all | bytes 2097152 | tf_op jit(solution)/shard_map/all_to_all | solution.py:246
  (47 shorter events, 9.0 us)
Async XLA Ops:
  0.0 29.4 %collective-permute-start.1 = (bf16[512,256]{1,0:T(8,128)(2,1)}, bf16[512,256]{1,0:T(8,128)(2,1)S(1)}, u32[]{:S(2)}, u32[]{:S(2)}) collective-permute-start(bf16[512,256]{1,0:T(8,128)(2,1)} %param.13), channel_id=1, source_target_pairs={{0,0},{1,32},{2,64},{3,96},{32,1},{33,33},{34,65},{35,97},{64,2},{... | collective-permute-start | bytes 786440 | tf_op jit(solution)/shard_map/ppermute | solution.py:193
  2.3 31.1 %copy-start.11 = (f32[8192,16]{0,1:T(8,128)S(1)}, f32[8192,16]{0,1:T(8,128)}, u32[]{:S(2)}) copy-start(f32[8192,16]{0,1:T(8,128)} %param.12) | copy-start | bytes 1572868
  2.4 8.9 %collective-permute-start = (bf16[3,2,512]{2,1,0:T(2,128)(2,1)S(1)}, bf16[3,2,512]{2,1,0:T(2,128)(2,1)S(1)}, u32[]{:S(2)}, u32[]{:S(2)}) collective-permute-start(bf16[3,2,512]{2,1,0:T(2,128)(2,1)S(1)} %slice.3), channel_id=1, source_target_pairs={{0,16},{16,32},{32,48},{48,64},{64,80},{80,96},{96,112},{112,128},... | collective-permute-start | bytes 18440 | tf_op jit(solution)/shard_map/ppermute | solution.py:192
  11.3 0.6 copy-start.15
  14.6 25.8 %all-to-all-start = ((bf16[32,16,256]{2,1,0:T(8,128)(2,1)}), bf16[32,16,256]{2,1,0:T(8,128)(2,1)S(1)}, u32[]{:S(2)}, u32[]{:S(2)}) async-start(bf16[32,16,256]{2,1,0:T(8,128)(2,1)} %get-tuple-element.9.refs_0_), calls=%async_computation | async-start | bytes 524288 | tf_op jit(solution)/shard_map/all_to_all | solution.py:201
  29.4 0.7 copy-start.10
  30.1 10.3 %collective-permute-start.2 = (bf16[512,256]{1,0:T(8,128)(2,1)}, bf16[512,256]{1,0:T(8,128)(2,1)S(1)}, u32[]{:S(2)}, u32[]{:S(2)}) collective-permute-start(bf16[512,256]{1,0:T(8,128)(2,1)} %shard_map.103.own), channel_id=1, source_target_pairs={{0,256},{256,0},{1,257},{257,1},{2,258},{258,2},{3,259},{259,3},{4... | collective-permute-start | bytes 786440 | tf_op jit(solution)/shard_map/ppermute | solution.py:206
  40.4 0.7 copy-start.9
  41.1 0.7 copy-start.13
  43.7 6.8 %collective-permute-start.3 = (bf16[2,512,256]{2,1,0:T(8,128)(2,1)}, bf16[2,512,256]{2,1,0:T(8,128)(2,1)S(1)}, u32[]{:S(2)}, u32[]{:S(2)}) collective-permute-start(bf16[2,512,256]{2,1,0:T(8,128)(2,1)} %shard_map.104.dep.own), channel_id=1, source_target_pairs={{0,16},{16,0},{1,17},{17,1},{2,18},{18,2},{3,19},{19,3},{4,20},{20... | collective-permute-start | bytes 1572872 | tf_op jit(solution)/shard_map/ppermute | solution.py:214
  50.5 0.8 copy-start.12
  53.5 26.0 %collective-permute-start.4 = (bf16[2,512,512]{2,1,0:T(8,128)(2,1)}, bf16[2,512,512]{2,1,0:T(8,128)(2,1)S(1)}, u32[]{:S(2)}, u32[]{:S(2)}) collective-permute-start(bf16[2,512,512]{2,1,0:T(8,128)(2,1)} %shard_map.106.refs_0_.w0), channel_id=1, source_target_pairs={{0,32},{16,240},{32,64},{48,16},{64,96},{80,48},{96,128},{112,80},... | collective-permute-start | bytes 3145736 | tf_op jit(solution)/shard_map/ppermute | solution.py:169
  62.4 23.0 %all-to-all-start.1 = ((bf16[32,16,256]{2,1,0:T(8,128)(2,1)}), bf16[32,16,256]{2,1,0:T(8,128)(2,1)S(1)}, u32[]{:S(2)}, u32[]{:S(2)}) async-start(bf16[32,16,256]{2,1,0:T(8,128)(2,1)} %shard_map.107.refs_0_), calls=%async_computation.1 | async-start | bytes 524288 | tf_op jit(solution)/shard_map/all_to_all | solution.py:224
  79.5 1.0 copy-start.5
  80.5 17.0 %collective-permute-start.5 = (bf16[2,512,512]{2,1,0:T(8,128)(2,1)}, bf16[2,512,512]{2,1,0:T(8,128)(2,1)S(1)}, u32[]{:S(2)}, u32[]{:S(2)}) collective-permute-start(bf16[2,512,512]{2,1,0:T(8,128)(2,1)} %shard_map.109.w1), channel_id=1, source_target_pairs={{0,32},{16,240},{32,64},{48,16},{64,96},{80,48},{96,128},{112,80},... | collective-permute-start | bytes 3145736 | tf_op jit(solution)/shard_map/ppermute | solution.py:169
  85.4 0.7 copy-start.14
  88.4 33.2 %all-to-all-start.2 = ((bf16[4,256,512]{2,1,0:T(8,128)(2,1)}), bf16[4,256,512]{2,1,0:T(8,128)(2,1)S(1)}, u32[]{:S(2)}, u32[]{:S(2)}) async-start(bf16[4,256,512]{2,1,0:T(8,128)(2,1)} %shard_map.108.refs_0_), calls=%async_computation.2 | async-start | bytes 2097152 | tf_op jit(solution)/shard_map/all_to_all | solution.py:234
  97.4 1.0 copy-start.1
  98.5 17.2 %collective-permute-start.6 = (bf16[2,512,512]{2,1,0:T(8,128)(2,1)}, bf16[2,512,512]{2,1,0:T(8,128)(2,1)S(1)}, u32[]{:S(2)}, u32[]{:S(2)}) collective-permute-start(bf16[2,512,512]{2,1,0:T(8,128)(2,1)} %shard_map.110.w2), channel_id=1, source_target_pairs={{0,32},{16,240},{32,64},{48,16},{64,96},{80,48},{96,128},{112,80},... | collective-permute-start | bytes 3145736 | tf_op jit(solution)/shard_map/ppermute | solution.py:169
  115.7 6.8 %copy-start.7 = (bf16[2,512,512]{2,1,0:T(8,128)(2,1)}, bf16[2,512,512]{2,1,0:T(8,128)(2,1)S(1)}, u32[]{:S(2)}) copy-start(bf16[2,512,512]{2,1,0:T(8,128)(2,1)S(1)} %collective-permute-done.6.w3) | copy-start | bytes 3145732
  116.6 11.3 %collective-permute-start.8 = (bf16[512,512]{1,0:T(8,128)(2,1)}, bf16[512,512]{1,0:T(8,128)(2,1)}, u32[]{:S(2)}, u32[]{:S(2)}) collective-permute-start(bf16[512,512]{1,0:T(8,128)(2,1)} %dynamic-slice_bitcast_fusion.refs_0_), channel_id=1, source_target_pairs={{0,32},{16,240},{32,64},{48,16},{64,96},{80,48},{96,128},{112,80},... | collective-permute-start | bytes 1572872 | tf_op jit(solution)/shard_map/ppermute | solution.py:169
  121.6 1.0 copy-start.3
  122.6 5.4 %collective-permute-start.7 = (bf16[4,256,512]{2,1,0:T(8,128)(2,1)}, bf16[4,256,512]{2,1,0:T(8,128)(2,1)}, u32[]{:S(2)}, u32[]{:S(2)}) collective-permute-start(bf16[4,256,512]{2,1,0:T(8,128)(2,1)} %shard_map.111.g_own), channel_id=1, source_target_pairs={{0,16},{16,0},{1,17},{17,1},{2,18},{18,2},{3,19},{19,3},{4,20},{20... | collective-permute-start | bytes 3145736 | tf_op jit(solution)/shard_map/ppermute | solution.py:236
  124.6 3.4 %copy-start = (bf16[2,512,512]{2,1,0:T(8,128)(2,1)S(1)}, bf16[2,512,512]{2,1,0:T(8,128)(2,1)}, u32[]{:S(2)}) copy-start(bf16[2,512,512]{2,1,0:T(8,128)(2,1)} %shard_map.106.refs_0_.w0) | copy-start | bytes 3145732
  124.6 3.4 %copy-start.2 = (bf16[2,512,512]{2,1,0:T(8,128)(2,1)S(1)}, bf16[2,512,512]{2,1,0:T(8,128)(2,1)}, u32[]{:S(2)}) copy-start(bf16[2,512,512]{2,1,0:T(8,128)(2,1)} %shard_map.110.w2) | copy-start | bytes 3145732
  124.6 3.4 %copy-start.4 = (bf16[4,256,512]{2,1,0:T(8,128)(2,1)S(1)}, bf16[4,256,512]{2,1,0:T(8,128)(2,1)}, u32[]{:S(2)}) copy-start(bf16[4,256,512]{2,1,0:T(8,128)(2,1)} %shard_map.111.g_own) | copy-start | bytes 3145732
  128.0 1.2 copy-start.6
  129.2 1.2 copy-start.8
  134.6 8.1 %collective-permute-start.9 = (bf16[4,256,512]{2,1,0:T(8,128)(2,1)S(1)}, bf16[4,256,512]{2,1,0:T(8,128)(2,1)S(1)}, u32[]{:S(2)}, u32[]{:S(2)}) collective-permute-start(bf16[4,256,512]{2,1,0:T(8,128)(2,1)S(1)} %get-tuple-element.12), channel_id=1, source_target_pairs={{0,16},{16,0},{1,17},{17,1},{2,18},{18,2},{3,19},{19,3},{4,20},{20... | collective-permute-start | bytes 3145736 | tf_op jit(solution)/shard_map/ppermute | solution.py:245

commit v3 on v2

--- a/solution.py
+++ b/solution.py
@@ -128,22 +128,39 @@
     out[:, :, WIDE:] = other[...]
 
 
-def project_kernel(place, g_own, g_other, w0, w1, w2, w3, w4, keep, send, total):
+def project_kernel(
+    place, g_own, other_ref, w0, w1_ref, w2, w3_ref, w4_ref, keep, send, g_other, w1, w3, w4, total, sems
+):
     yl, z, core = place[0], place[1], place[2]
+    mine = lax.rem(yl + core, 2)
+    pairs = ((w1_ref, w1), (w3_ref, w3), (other_ref, g_other), (w4_ref, w4))
+    copies = [pltpu.make_async_copy(a, b, sems.at[i]) for i, (a, b) in enumerate(pairs)]
+    for copy in copies:
+        copy.start()
     total[...] = jnp.zeros_like(total)
 
-    def add(step, row, block):
+    def add(tokens, step, row, block):
         source = (z + 8 + step * (2 * core - 1)) % 8
-        group = 2 * row + source // 4
-        total[group, 0] += dot(g_own[source % 4], block)
-        total[group, 1] += dot(g_other[source % 4], block)
-
-    mine = lax.rem(yl + core, 2)
-    add(0, mine, w0[core])
+        rows = g_other if tokens else g_own
+        total[2 * row + source // 4, tokens] += dot(rows[source % 4], block)
+
+    def both(tokens, step, ref):
+        add(tokens, step, yl, ref[0])
+        add(tokens, step, 1 - yl, ref[1])
+
+    add(0, 0, mine, w0[core])
+    both(0, 2, w2)
+    copies[0].wait()
+    both(0, 1, w1)
+    copies[1].wait()
+    both(0, 3, w3)
+    copies[2].wait()
+    add(1, 0, mine, w0[core])
     for step, ref in ((1, w1), (2, w2), (3, w3)):
-        add(step, yl, ref[0])
-        add(step, 1 - yl, ref[1])
-    add(4, mine, w4[...])
+        both(1, step, ref)
+    copies[3].wait()
+    for tokens in range(2):
+        add(tokens, 4, mine, w4[...])
 
     own = pl.ds(pl.multiple_of(core * WIDE, WIDE), WIDE)
     other = pl.ds(pl.multiple_of((1 - core) * WIDE, WIDE), WIDE)
@@ -220,13 +237,11 @@
     )
     w1 = along(w0)
     convolved, = tie(w0, convolved)
-    w1, = tie(convolved, w1)
     convolved = lax.all_to_all(convolved, CTX, split_axis=0, concat_axis=0, tiled=True)
     w2 = along(w1)
     gated = call(
         gate_kernel, jax.ShapeDtypeStruct((4, rows, width), BF16), 0, 2, flops=6 * 10**9
     )(convolved, query)
-    w2, = tie(gated, w2)
     w3 = along(w2)
     half = lax.dynamic_index_in_dim(w3, core, 0, keepdims=False)
     w4, = tie(half, along(half), flops=10**10)
@@ -235,12 +250,21 @@
     g_own, = tie(half, g_own, flops=10**10)
     g_other = lax.ppermute(g_own, "c", ring(2, 1))
 
-    keep, send = call(
+    keep, send = pl.pallas_call(
         project_kernel,
-        [jax.ShapeDtypeStruct((4, rows, width), BF16)] * 2,
-        1, 7,
-        [pltpu.VMEM((4, 2, rows, width), F32)],
-        vmem=24,
+        out_shape=[jax.ShapeDtypeStruct((4, rows, width), BF16)] * 2,
+        in_specs=[SMEM, VMEM, ANY, VMEM, ANY, VMEM, ANY, ANY],
+        out_specs=[VMEM] * 2,
+        scratch_shapes=[
+            pltpu.VMEM((4, rows, width), BF16),
+            pltpu.VMEM((2, width, width), BF16),
+            pltpu.VMEM((2, width, width), BF16),
+            pltpu.VMEM((width, width), BF16),
+            pltpu.VMEM((4, 2, rows, width), F32),
+            pltpu.SemaphoreType.DMA((4,)),
+        ],
+        compiler_params=pltpu.CompilerParams(vmem_limit_bytes=24 * MIB),
+        cost_estimate=pl.CostEstimate(flops=1000, bytes_accessed=1000, transcendentals=0),
     )(place, g_own, g_other, w0, w1, w2, w3, w4)
     partial = (keep.astype(F32) + lax.ppermute(send, "c", ring(2, 1)).astype(F32)).astype(BF16)
     parts = lax.all_to_all(partial, "x", split_axis=0, concat_axis=0, tiled=True)

time: 163 us -> 161 us (0.988)
  local copies, waits for them, and re-layouts: 12.2 us -> 8.86 us
    unnamed x32 -> x24, local copies, waits for them, and re-layouts: 9.63 us -> 6.41 us
  transfers between devices with their start and end apart: 13 -> 13, of which waited for: 7 -> 7; matrix products, arithmetic and copies ran while one was open for 2% -> 2% of each run, Pallas kernels for 8% -> 9%
where the time goes in v3:
time: 161 us; the launch traced here: 159 us
  starting transfers between devices  68.9 us (43%)
  waiting for transfers between devices  39.5 us (25%)
  Pallas kernels  22.6 us (14%)
  blocking collectives  18.1 us (11%)
  local copies, waits for them, and re-layouts  8.86 us (6%)
    ppermute x4, waiting for transfers between devices, along(): return lax.ppermute(a, ('z', 'c'), pairs)  33.4 us
    ppermute x4, starting transfers between devices, along(): return lax.ppermute(a, ('z', 'c'), pairs)  24 us
    all_to_all x1, blocking collectives, shards(): lax.all_to_all(partial, 'x', split_axis=0, concat_axis=0, tiled=True)  18.1 us
    all_to_all x1, starting transfers between devices, shards(): signal = lax.all_to_all(mixed, CTX, split_axis=0, concat_axis=0, tiled=True)  14.8 us
    ppermute x1, starting transfers between devices, shards(): lead = lax.ppermute(projected[:, -2:], CTX, order)  7.51 us
    unnamed x24, local copies, waits for them, and re-layouts  6.41 us
    ppermute x1, starting transfers between devices, shards(): lax.ppermute(send, 'c', ring(2, 1)).astype(F32)  5.96 us
    pallas_call x1, Pallas kernels, shards(): pl.pallas_call(project_kernel, out_shape=[jax.ShapeDtypeStruct((4, rows,...  4.9 us
  transfers between devices with their start and end apart: 13, of which 7 were waited for; matrix products, arithmetic and copies ran while one was open for 2% of the time, Pallas kernels for 9%

profile of v3, /device:TPU:1, one launch (start us, length us, event | category | flops | bytes accessed | tf_op | source)
XLA Modules:
  0.0 159.4 jit_solution(5011532480534715850)
XLA Ops:
  0.0 1.6 %collective-permute-start.1 = (bf16[512,256]{1,0:T(8,128)(2,1)}, bf16[512,256]{1,0:T(8,128)(2,1)S(1)}, u32[]{:S(2)}, u32[]{:S(2)}) collective-permute-start(bf16[512,256]{1,0:T(8,128)(2,1)} %param.13), channel_id=1, source_target_pairs={{0,0},{1,32},{2,64},{3,96},{32,1},{33,33},{34,65},{35,97},{64,2},{... | collective-permute-start | bytes 786440 | tf_op jit(solution)/shard_map/ppermute | solution.py:210
  2.4 7.5 %collective-permute-start = (bf16[3,2,512]{2,1,0:T(2,128)(2,1)S(1)}, bf16[3,2,512]{2,1,0:T(2,128)(2,1)S(1)}, u32[]{:S(2)}, u32[]{:S(2)}) collective-permute-start(bf16[3,2,512]{2,1,0:T(2,128)(2,1)S(1)} %slice.3), channel_id=1, source_target_pairs={{0,16},{16,32},{32,48},{48,64},{64,80},{80,96},{96,112},{112,128},... | collective-permute-start | bytes 18440 | tf_op jit(solution)/shard_map/ppermute | solution.py:209
  9.9 1.4 collective-permute-done.lead
  11.9 2.7 %shard_map.100 = (bf16[32,16,256]{2,1,0:T(8,128)(2,1)}, f32[512,256]{1,0:T(8,128)}) custom-call(bf16[3,256,512]{2,1,0:T(8,128)(2,1)} %projected.1, bf16[3,2,512]{2,1,0:T(2,128)(2,1)} %copy-done.11, f32[3,3,512]{2,1,0:T(4,128)} %weight.1), custom_call_target="tpu_custom_call" | custom-call | flops 1000 | bytes 1000 | tf_op jit(solution)/shard_map/pallas_call | solution.py:212
  14.6 14.8 %all-to-all-start = ((bf16[32,16,256]{2,1,0:T(8,128)(2,1)}), bf16[32,16,256]{2,1,0:T(8,128)(2,1)S(1)}, u32[]{:S(2)}, u32[]{:S(2)}) async-start(bf16[32,16,256]{2,1,0:T(8,128)(2,1)} %get-tuple-element.9.refs_0_), calls=%async_computation | async-start | bytes 524288 | tf_op jit(solution)/shard_map/all_to_all | solution.py:218
  30.1 3.3 %collective-permute-start.2 = (bf16[512,256]{1,0:T(8,128)(2,1)}, bf16[512,256]{1,0:T(8,128)(2,1)S(1)}, u32[]{:S(2)}, u32[]{:S(2)}) collective-permute-start(bf16[512,256]{1,0:T(8,128)(2,1)} %shard_map.103.own), channel_id=1, source_target_pairs={{0,256},{256,0},{1,257},{257,1},{2,258},{258,2},{3,259},{259,3},{4... | collective-permute-start | bytes 786440 | tf_op jit(solution)/shard_map/ppermute | solution.py:223
  33.4 0.9 copy.19
  34.3 3.8 %shard_map.102.spectrum = f32[512,512]{1,0:T(8,128)} custom-call(f32[32,16,256]{2,1,0:T(8,128)} %shard_map.101.taps, bf16[1024,512]{1,0:T(8,128)(2,1)} %constant.37.clone.first, f32[32,1,256]{2,1,0:T(1,128)} %constant.38.clone.cos, f32[32,1,256]{2,1,0:T(1,128)} %constant.39.clone.sin, bf16[512,512]{1,0:T(8,128)(2,1)} %constant.40.clone.fwd), custom_call_target="tpu_custom_call" | custom-call | flops 1000 | bytes 1000 | tf_op jit(solution)/shard_map/pallas_call | solution.py:224
  38.0 2.3 %all-to-all-done.signal = bf16[32,16,256]{2,1,0:T(8,128)(2,1)S(1)} async-done(((bf16[32,16,256]{2,1,0:T(8,128)(2,1)}), bf16[32,16,256]{2,1,0:T(8,128)(2,1)S(1)}, u32[]{:S(2)}, u32[]{:S(2)}) %all-to-all-start) | async-done | bytes 262176 | tf_op jit(solution)/shard_map/all_to_all | solution.py:218
  41.8 1.9 %shard_map.104.dep.own = bf16[2,512,256]{2,1,0:T(8,128)(2,1)} custom-call(bf16[32,16,256]{2,1,0:T(8,128)(2,1)} %copy-done.5, f32[512,512]{1,0:T(8,128)} %shard_map.102.spectrum, bf16[512,256]{1,0:T(8,128)(2,1)} %shard_map.103.own, bf16[512,256]{1,0:T(8,128)(2,1)} %copy-done.9), custom_call_target="tpu_custom_call" | custom-call | flops 1000 | bytes 1000 | tf_op jit(solution)/shard_map/pallas_call | solution.py:228
  43.7 1.9 %collective-permute-start.3 = (bf16[2,512,256]{2,1,0:T(8,128)(2,1)}, bf16[2,512,256]{2,1,0:T(8,128)(2,1)S(1)}, u32[]{:S(2)}, u32[]{:S(2)}) collective-permute-start(bf16[2,512,256]{2,1,0:T(8,128)(2,1)} %shard_map.104.dep.own), channel_id=1, source_target_pairs={{0,16},{16,0},{1,17},{17,1},{2,18},{18,2},{3,19},{19,3},{4,20},{20... | collective-permute-start | bytes 1572872 | tf_op jit(solution)/shard_map/ppermute | solution.py:231
  45.6 4.9 %shard_map.105.dep.refs_1_ = bf16[32,16,256]{2,1,0:T(8,128)(2,1)} custom-call(bf16[2,512,256]{2,1,0:T(8,128)(2,1)} %shard_map.104.dep.own, bf16[32,16,256]{2,1,0:T(8,128)(2,1)} %copy-done.5, f32[512,512]{1,0:T(8,128)} %shard_map.102.spectrum, bf16[1024,512]{1,0:T(8,128)(2,1)} %constant.37.clone.first, f32[32,1,256]{2,1,0:T(1,128)} %constant.38.clone.cos, ...), custom_call_target="tpu_custom_call" | custom-call | flops 1000 | bytes 1000 | tf_op jit(solution)/shard_map/pallas_call | solution.py:232
  51.3 2.3 %shard_map.106.refs_0_.w0 = bf16[2,512,512]{2,1,0:T(8,128)(2,1)} custom-call(bf16[32,16,256]{2,1,0:T(8,128)(2,1)} %shard_map.105.dep.refs_1_, bf16[2,512,256]{2,1,0:T(8,128)(2,1)} %shard_map.104.dep.own, bf16[2,512,256]{2,1,0:T(8,128)(2,1)} %copy-done.8), custom_call_target="tpu_custom_call" | custom-call | flops 1000 | bytes 1000 | tf_op jit(solution)/shard_map/pallas_call | solution.py:235
  53.5 8.9 %collective-permute-start.4 = (bf16[2,512,512]{2,1,0:T(8,128)(2,1)}, bf16[2,512,512]{2,1,0:T(8,128)(2,1)S(1)}, u32[]{:S(2)}, u32[]{:S(2)}) collective-permute-start(bf16[2,512,512]{2,1,0:T(8,128)(2,1)} %shard_map.106.refs_0_.w0), channel_id=1, source_target_pairs={{0,32},{16,240},{32,64},{48,16},{64,96},{80,48},{96,128},{112,80},... | collective-permute-start | bytes 3145736 | tf_op jit(solution)/shard_map/ppermute | solution.py:186
  62.4 4.4 %all-to-all-start.1 = ((bf16[32,16,256]{2,1,0:T(8,128)(2,1)}), bf16[32,16,256]{2,1,0:T(8,128)(2,1)S(1)}, u32[]{:S(2)}, u32[]{:S(2)}) async-start(bf16[32,16,256]{2,1,0:T(8,128)(2,1)} %shard_map.107), calls=%async_computation.1 | async-start | bytes 524288 | tf_op jit(solution)/shard_map/all_to_all | solution.py:240
  66.8 12.7 %collective-permute-done.4.w1_ref = bf16[2,512,512]{2,1,0:T(8,128)(2,1)S(1)} collective-permute-done((bf16[2,512,512]{2,1,0:T(8,128)(2,1)}, bf16[2,512,512]{2,1,0:T(8,128)(2,1)S(1)}, u32[]{:S(2)}, u32[]{:S(2)}) %collective-permute-start.4) | collective-permute-done | bytes 1048608 | tf_op jit(solution)/shard_map/ppermute | solution.py:186
  79.5 4.9 %collective-permute-start.5 = (bf16[2,512,512]{2,1,0:T(8,128)(2,1)S(1)}, bf16[2,512,512]{2,1,0:T(8,128)(2,1)}, u32[]{:S(2)}, u32[]{:S(2)}) collective-permute-start(bf16[2,512,512]{2,1,0:T(8,128)(2,1)S(1)} %collective-permute-done.4.w1_ref), channel_id=1, source_target_pairs={{0,32},{16,240},{32,64},{48,16},{64,96},{80,48},{96,128},{112,80},... | collective-permute-start | bytes 3145736 | tf_op jit(solution)/shard_map/ppermute | solution.py:186
  85.2 2.2 %shard_map.108 = bf16[4,256,512]{2,1,0:T(8,128)(2,1)} custom-call(bf16[32,16,256]{2,1,0:T(8,128)(2,1)} %copy-done.10, f32[512,256]{1,0:T(8,128)} %get-tuple-element.10.query), custom_call_target="tpu_custom_call" | custom-call | flops 6000000000 | bytes 1000 | tf_op jit(solution)/shard_map/pallas_call | solution.py:242
  87.4 3.5 %all-to-all-start.2 = ((bf16[4,256,512]{2,1,0:T(8,128)(2,1)}), bf16[4,256,512]{2,1,0:T(8,128)(2,1)S(1)}, u32[]{:S(2)}, u32[]{:S(2)}) async-start(bf16[4,256,512]{2,1,0:T(8,128)(2,1)} %shard_map.108), calls=%async_computation.2 | async-start | bytes 2097152 | tf_op jit(solution)/shard_map/all_to_all | solution.py:249
  90.9 5.2 %collective-permute-done.5.w2 = bf16[2,512,512]{2,1,0:T(8,128)(2,1)} collective-permute-done((bf16[2,512,512]{2,1,0:T(8,128)(2,1)S(1)}, bf16[2,512,512]{2,1,0:T(8,128)(2,1)}, u32[]{:S(2)}, u32[]{:S(2)}) %collective-permute-start.5) | collective-permute-done | bytes 1048608 | tf_op jit(solution)/shard_map/ppermute | solution.py:186
  96.2 5.3 %collective-permute-start.6 = (bf16[2,512,512]{2,1,0:T(8,128)(2,1)}, bf16[2,512,512]{2,1,0:T(8,128)(2,1)S(1)}, u32[]{:S(2)}, u32[]{:S(2)}) collective-permute-start(bf16[2,512,512]{2,1,0:T(8,128)(2,1)} %collective-permute-done.5.w2), channel_id=1, source_target_pairs={{0,32},{16,240},{32,64},{48,16},{64,96},{80,48},{96,128},{112,80},... | collective-permute-start | bytes 3145736 | tf_op jit(solution)/shard_map/ppermute | solution.py:186
  101.5 12.0 %collective-permute-done.6.w3_ref = bf16[2,512,512]{2,1,0:T(8,128)(2,1)S(1)} collective-permute-done((bf16[2,512,512]{2,1,0:T(8,128)(2,1)}, bf16[2,512,512]{2,1,0:T(8,128)(2,1)S(1)}, u32[]{:S(2)}, u32[]{:S(2)}) %collective-permute-start.6) | collective-permute-done | bytes 1048608 | tf_op jit(solution)/shard_map/ppermute | solution.py:186
  114.4 4.9 %collective-permute-start.8 = (bf16[512,512]{1,0:T(8,128)(2,1)}, bf16[512,512]{1,0:T(8,128)(2,1)}, u32[]{:S(2)}, u32[]{:S(2)}) collective-permute-start(bf16[512,512]{1,0:T(8,128)(2,1)} %dynamic-slice_bitcast_fusion.refs_0_), channel_id=1, source_target_pairs={{0,32},{16,240},{32,64},{48,16},{64,96},{80,48},{96,128},{112,80},... | collective-permute-start | bytes 1572872 | tf_op jit(solution)/shard_map/ppermute | solution.py:186
  119.3 1.0 copy-done.1
  120.3 1.9 %collective-permute-start.7 = (bf16[4,256,512]{2,1,0:T(8,128)(2,1)}, bf16[4,256,512]{2,1,0:T(8,128)(2,1)}, u32[]{:S(2)}, u32[]{:S(2)}) collective-permute-start(bf16[4,256,512]{2,1,0:T(8,128)(2,1)} %shard_map.109.g_own), channel_id=1, source_target_pairs={{0,16},{16,0},{1,17},{17,1},{2,18},{18,2},{3,19},{19,3},{4,20},{20... | collective-permute-start | bytes 3145736 | tf_op jit(solution)/shard_map/ppermute | solution.py:251
  122.3 3.4 %collective-permute-done.8.refs_1_ = bf16[512,512]{1,0:T(8,128)(2,1)} collective-permute-done((bf16[512,512]{1,0:T(8,128)(2,1)}, bf16[512,512]{1,0:T(8,128)(2,1)}, u32[]{:S(2)}, u32[]{:S(2)}) %collective-permute-start.8) | collective-permute-done | bytes 524320 | tf_op jit(solution)/shard_map/ppermute | solution.py:186
  125.7 1.2 copy-done.4
  126.9 4.9 %shard_map.111 = (bf16[4,256,512]{2,1,0:T(8,128)(2,1)S(1)}, bf16[4,256,512]{2,1,0:T(8,128)(2,1)S(1)}) custom-call(s32[3]{0:T(128)S(1)} %pad_add_fusion.place, bf16[4,256,512]{2,1,0:T(8,128)(2,1)S(1)} %copy-done.2, bf16[4,256,512]{2,1,0:T(8,128)(2,1)} %collective-permute-done.7.other_ref, bf16[2,512,512]{2,1,0:T(8,128)(2,1)S(1)} %copy-done, ...), custom_call_target="tpu_custom_call" | custom-call | flops 1000 | bytes 1000 | tf_op jit(solution)/shard_map/pallas_call | solution.py:253
  131.8 6.0 %collective-permute-start.9 = (bf16[4,256,512]{2,1,0:T(8,128)(2,1)S(1)}, bf16[4,256,512]{2,1,0:T(8,128)(2,1)S(1)}, u32[]{:S(2)}, u32[]{:S(2)}) collective-permute-start(bf16[4,256,512]{2,1,0:T(8,128)(2,1)S(1)} %get-tuple-element.12), channel_id=1, source_target_pairs={{0,16},{16,0},{1,17},{17,1},{2,18},{18,2},{3,19},{19,3},{4,20},{20... | collective-permute-start | bytes 3145736 | tf_op jit(solution)/shard_map/ppermute | solution.py:269
  137.8 2.3 %collective-permute-done.9 = bf16[4,256,512]{2,1,0:T(8,128)(2,1)S(1)} collective-permute-done((bf16[4,256,512]{2,1,0:T(8,128)(2,1)S(1)}, bf16[4,256,512]{2,1,0:T(8,128)(2,1)S(1)}, u32[]{:S(2)}, u32[]{:S(2)}) %collective-permute-start.9) | collective-permute-done | bytes 1048608 | tf_op jit(solution)/shard_map/ppermute | solution.py:269
  140.4 18.1 %all_to_all.20 = bf16[4,256,512]{2,1,0:T(8,128)(2,1)S(1)} all-to-all(bf16[4,256,512]{2,1,0:T(8,128)(2,1)S(1)} %add_convert_fusion), channel_id=1, replica_groups=mesh['yl'=2,'z'=8,'c'=2,'x'=4,'yh'=4] {'x'}, dimensions={0} | all-to-all | bytes 2097152 | tf_op jit(solution)/shard_map/all_to_all | solution.py:270
  158.4 0.9 reduce_sum.12
  (37 shorter events, 6.2 us)
Async XLA Ops:
  0.0 29.4 %collective-permute-start.1 = (bf16[512,256]{1,0:T(8,128)(2,1)}, bf16[512,256]{1,0:T(8,128)(2,1)S(1)}, u32[]{:S(2)}, u32[]{:S(2)}) collective-permute-start(bf16[512,256]{1,0:T(8,128)(2,1)} %param.13), channel_id=1, source_target_pairs={{0,0},{1,32},{2,64},{3,96},{32,1},{33,33},{34,65},{35,97},{64,2},{... | collective-permute-start | bytes 786440 | tf_op jit(solution)/shard_map/ppermute | solution.py:210
  2.3 31.0 %copy-start.7 = (f32[8192,16]{0,1:T(8,128)S(1)}, f32[8192,16]{0,1:T(8,128)}, u32[]{:S(2)}) copy-start(f32[8192,16]{0,1:T(8,128)} %param.12) | copy-start | bytes 1572868
  2.4 8.9 %collective-permute-start = (bf16[3,2,512]{2,1,0:T(2,128)(2,1)S(1)}, bf16[3,2,512]{2,1,0:T(2,128)(2,1)S(1)}, u32[]{:S(2)}, u32[]{:S(2)}) collective-permute-start(bf16[3,2,512]{2,1,0:T(2,128)(2,1)S(1)} %slice.3), channel_id=1, source_target_pairs={{0,16},{16,32},{32,48},{48,64},{64,80},{80,96},{96,112},{112,128},... | collective-permute-start | bytes 18440 | tf_op jit(solution)/shard_map/ppermute | solution.py:209
  11.3 0.6 copy-start.11
  14.6 25.8 %all-to-all-start = ((bf16[32,16,256]{2,1,0:T(8,128)(2,1)}), bf16[32,16,256]{2,1,0:T(8,128)(2,1)S(1)}, u32[]{:S(2)}, u32[]{:S(2)}) async-start(bf16[32,16,256]{2,1,0:T(8,128)(2,1)} %get-tuple-element.9.refs_0_), calls=%async_computation | async-start | bytes 524288 | tf_op jit(solution)/shard_map/all_to_all | solution.py:218
  29.4 0.7 copy-start.6
  30.1 10.3 %collective-permute-start.2 = (bf16[512,256]{1,0:T(8,128)(2,1)}, bf16[512,256]{1,0:T(8,128)(2,1)S(1)}, u32[]{:S(2)}, u32[]{:S(2)}) collective-permute-start(bf16[512,256]{1,0:T(8,128)(2,1)} %shard_map.103.own), channel_id=1, source_target_pairs={{0,256},{256,0},{1,257},{257,1},{2,258},{258,2},{3,259},{259,3},{4... | collective-permute-start | bytes 786440 | tf_op jit(solution)/shard_map/ppermute | solution.py:223
  40.4 0.7 copy-start.5
  41.1 0.7 copy-start.9
  43.7 6.8 %collective-permute-start.3 = (bf16[2,512,256]{2,1,0:T(8,128)(2,1)}, bf16[2,512,256]{2,1,0:T(8,128)(2,1)S(1)}, u32[]{:S(2)}, u32[]{:S(2)}) collective-permute-start(bf16[2,512,256]{2,1,0:T(8,128)(2,1)} %shard_map.104.dep.own), channel_id=1, source_target_pairs={{0,16},{16,0},{1,17},{17,1},{2,18},{18,2},{3,19},{19,3},{4,20},{20... | collective-permute-start | bytes 1572872 | tf_op jit(solution)/shard_map/ppermute | solution.py:231
  50.5 0.8 copy-start.8
  53.5 26.0 %collective-permute-start.4 = (bf16[2,512,512]{2,1,0:T(8,128)(2,1)}, bf16[2,512,512]{2,1,0:T(8,128)(2,1)S(1)}, u32[]{:S(2)}, u32[]{:S(2)}) collective-permute-start(bf16[2,512,512]{2,1,0:T(8,128)(2,1)} %shard_map.106.refs_0_.w0), channel_id=1, source_target_pairs={{0,32},{16,240},{32,64},{48,16},{64,96},{80,48},{96,128},{112,80},... | collective-permute-start | bytes 3145736 | tf_op jit(solution)/shard_map/ppermute | solution.py:186
  62.4 22.0 %all-to-all-start.1 = ((bf16[32,16,256]{2,1,0:T(8,128)(2,1)}), bf16[32,16,256]{2,1,0:T(8,128)(2,1)S(1)}, u32[]{:S(2)}, u32[]{:S(2)}) async-start(bf16[32,16,256]{2,1,0:T(8,128)(2,1)} %shard_map.107), calls=%async_computation.1 | async-start | bytes 524288 | tf_op jit(solution)/shard_map/all_to_all | solution.py:240
  79.5 7.9 %copy-start.3 = (bf16[2,512,512]{2,1,0:T(8,128)(2,1)}, bf16[2,512,512]{2,1,0:T(8,128)(2,1)S(1)}, u32[]{:S(2)}) copy-start(bf16[2,512,512]{2,1,0:T(8,128)(2,1)S(1)} %collective-permute-done.4.w1_ref) | copy-start | bytes 3145732
  79.5 16.6 %collective-permute-start.5 = (bf16[2,512,512]{2,1,0:T(8,128)(2,1)S(1)}, bf16[2,512,512]{2,1,0:T(8,128)(2,1)}, u32[]{:S(2)}, u32[]{:S(2)}) collective-permute-start(bf16[2,512,512]{2,1,0:T(8,128)(2,1)S(1)} %collective-permute-done.4.w1_ref), channel_id=1, source_target_pairs={{0,32},{16,240},{32,64},{48,16},{64,96},{80,48},{96,128},{112,80},... | collective-permute-start | bytes 3145736 | tf_op jit(solution)/shard_map/ppermute | solution.py:186
  84.5 0.7 copy-start.10
  87.4 31.9 %all-to-all-start.2 = ((bf16[4,256,512]{2,1,0:T(8,128)(2,1)}), bf16[4,256,512]{2,1,0:T(8,128)(2,1)S(1)}, u32[]{:S(2)}, u32[]{:S(2)}) async-start(bf16[4,256,512]{2,1,0:T(8,128)(2,1)} %shard_map.108), calls=%async_computation.2 | async-start | bytes 2097152 | tf_op jit(solution)/shard_map/all_to_all | solution.py:249
  96.2 17.4 %collective-permute-start.6 = (bf16[2,512,512]{2,1,0:T(8,128)(2,1)}, bf16[2,512,512]{2,1,0:T(8,128)(2,1)S(1)}, u32[]{:S(2)}, u32[]{:S(2)}) collective-permute-start(bf16[2,512,512]{2,1,0:T(8,128)(2,1)} %collective-permute-done.5.w2), channel_id=1, source_target_pairs={{0,32},{16,240},{32,64},{48,16},{64,96},{80,48},{96,128},{112,80},... | collective-permute-start | bytes 3145736 | tf_op jit(solution)/shard_map/ppermute | solution.py:186
  114.4 11.3 %collective-permute-start.8 = (bf16[512,512]{1,0:T(8,128)(2,1)}, bf16[512,512]{1,0:T(8,128)(2,1)}, u32[]{:S(2)}, u32[]{:S(2)}) collective-permute-start(bf16[512,512]{1,0:T(8,128)(2,1)} %dynamic-slice_bitcast_fusion.refs_0_), channel_id=1, source_target_pairs={{0,32},{16,240},{32,64},{48,16},{64,96},{80,48},{96,128},{112,80},... | collective-permute-start | bytes 1572872 | tf_op jit(solution)/shard_map/ppermute | solution.py:186
  119.3 1.0 copy-start.1
  120.3 5.4 %collective-permute-start.7 = (bf16[4,256,512]{2,1,0:T(8,128)(2,1)}, bf16[4,256,512]{2,1,0:T(8,128)(2,1)}, u32[]{:S(2)}, u32[]{:S(2)}) collective-permute-start(bf16[4,256,512]{2,1,0:T(8,128)(2,1)} %shard_map.109.g_own), channel_id=1, source_target_pairs={{0,16},{16,0},{1,17},{17,1},{2,18},{18,2},{3,19},{19,3},{4,20},{20... | collective-permute-start | bytes 3145736 | tf_op jit(solution)/shard_map/ppermute | solution.py:251
  122.3 3.4 %copy-start = (bf16[2,512,512]{2,1,0:T(8,128)(2,1)S(1)}, bf16[2,512,512]{2,1,0:T(8,128)(2,1)}, u32[]{:S(2)}) copy-start(bf16[2,512,512]{2,1,0:T(8,128)(2,1)} %shard_map.106.refs_0_.w0) | copy-start | bytes 3145732
  122.3 3.4 %copy-start.2 = (bf16[4,256,512]{2,1,0:T(8,128)(2,1)S(1)}, bf16[4,256,512]{2,1,0:T(8,128)(2,1)}, u32[]{:S(2)}) copy-start(bf16[4,256,512]{2,1,0:T(8,128)(2,1)} %shard_map.109.g_own) | copy-start | bytes 3145732
  125.7 1.2 copy-start.4
  131.8 8.2 %collective-permute-start.9 = (bf16[4,256,512]{2,1,0:T(8,128)(2,1)S(1)}, bf16[4,256,512]{2,1,0:T(8,128)(2,1)S(1)}, u32[]{:S(2)}, u32[]{:S(2)}) collective-permute-start(bf16[4,256,512]{2,1,0:T(8,128)(2,1)S(1)} %get-tuple-element.12), channel_id=1, source_target_pairs={{0,16},{16,0},{1,17},{17,1},{2,18},{18,2},{3,19},{19,3},{4,20},{20... | collective-permute-start | bytes 3145736 | tf_op jit(solution)/shard_map/ppermute | solution.py:269

commit v4 on v3

--- a/solution.py
+++ b/solution.py
@@ -194,6 +194,7 @@
         in_specs=[ANY] * (n + 1),
         out_specs=[ANY] * n,
         input_output_aliases={i + 1: i for i in range(n)},
+        compiler_params=pltpu.CompilerParams(vmem_limit_bytes=MIB),
         cost_estimate=pl.CostEstimate(flops=flops, bytes_accessed=1000, transcendentals=0),
     )(dep, *arrays)
 

time: 161 us -> 160 us (level)
  transfers between devices with their start and end apart: 13 -> 13, of which waited for: 7 -> 7; matrix products, arithmetic and copies ran while one was open for 2% -> 1% of each run, Pallas kernels for 9% -> 9%
where the time goes in v4:
time: 160 us; the launch traced here: 158 us
  starting transfers between devices  69.2 us (43%)
  waiting for transfers between devices  38.8 us (24%)
  Pallas kernels  22.7 us (14%)
  blocking collectives  18 us (11%)
  local copies, waits for them, and re-layouts  8.12 us (5%)
    ppermute x4, waiting for transfers between devices, along(): return lax.ppermute(a, ('z', 'c'), pairs)  33.1 us
    ppermute x4, starting transfers between devices, along(): return lax.ppermute(a, ('z', 'c'), pairs)  24.2 us
    all_to_all x1, blocking collectives, shards(): lax.all_to_all(partial, 'x', split_axis=0, concat_axis=0, tiled=True)  18 us
    all_to_all x1, starting transfers between devices, shards(): signal = lax.all_to_all(mixed, CTX, split_axis=0, concat_axis=0, tiled=True)  14.8 us
    ppermute x1, starting transfers between devices, shards(): lead = lax.ppermute(projected[:, -2:], CTX, order)  7.51 us
    unnamed x24, local copies, waits for them, and re-layouts  6.49 us
    ppermute x1, starting transfers between devices, shards(): lax.ppermute(send, 'c', ring(2, 1)).astype(F32)  5.98 us
    pallas_call x1, Pallas kernels, shards(): pl.pallas_call(project_kernel, out_shape=[jax.ShapeDtypeStruct((4, rows,...  4.95 us
  transfers between devices with their start and end apart: 13, of which 7 were waited for; matrix products, arithmetic and copies ran while one was open for 1% of the time, Pallas kernels for 9%

profile of v4, /device:TPU:1, one launch (start us, length us, event | category | flops | bytes accessed | tf_op | source)
XLA Modules:
  0.0 158.3 jit_solution(7907849370249009146)
XLA Ops:
  0.0 1.6 %collective-permute-start.1 = (bf16[512,256]{1,0:T(8,128)(2,1)}, bf16[512,256]{1,0:T(8,128)(2,1)S(1)}, u32[]{:S(2)}, u32[]{:S(2)}) collective-permute-start(bf16[512,256]{1,0:T(8,128)(2,1)} %param.13), channel_id=1, source_target_pairs={{0,0},{1,32},{2,64},{3,96},{32,1},{33,33},{34,65},{35,97},{64,2},{... | collective-permute-start | bytes 786440 | tf_op jit(solution)/shard_map/ppermute | solution.py:211
  2.4 7.5 %collective-permute-start = (bf16[3,2,512]{2,1,0:T(2,128)(2,1)S(1)}, bf16[3,2,512]{2,1,0:T(2,128)(2,1)S(1)}, u32[]{:S(2)}, u32[]{:S(2)}) collective-permute-start(bf16[3,2,512]{2,1,0:T(2,128)(2,1)S(1)} %slice.3), channel_id=1, source_target_pairs={{0,16},{16,32},{32,48},{48,64},{64,80},{80,96},{96,112},{112,128},... | collective-permute-start | bytes 18440 | tf_op jit(solution)/shard_map/ppermute | solution.py:210
  9.9 1.4 collective-permute-done.lead
  11.9 2.7 %shard_map.100 = (bf16[32,16,256]{2,1,0:T(8,128)(2,1)}, f32[512,256]{1,0:T(8,128)}) custom-call(bf16[3,256,512]{2,1,0:T(8,128)(2,1)} %projected.1, bf16[3,2,512]{2,1,0:T(2,128)(2,1)} %copy-done.11, f32[3,3,512]{2,1,0:T(4,128)} %weight.1), custom_call_target="tpu_custom_call" | custom-call | flops 1000 | bytes 1000 | tf_op jit(solution)/shard_map/pallas_call | solution.py:213
  14.6 14.8 %all-to-all-start = ((bf16[32,16,256]{2,1,0:T(8,128)(2,1)}), bf16[32,16,256]{2,1,0:T(8,128)(2,1)S(1)}, u32[]{:S(2)}, u32[]{:S(2)}) async-start(bf16[32,16,256]{2,1,0:T(8,128)(2,1)} %get-tuple-element.9.refs_0_), calls=%async_computation | async-start | bytes 524288 | tf_op jit(solution)/shard_map/all_to_all | solution.py:219
  29.4 1.0 copy-done.3
  30.4 3.4 %collective-permute-start.2 = (bf16[512,256]{1,0:T(8,128)(2,1)S(1)}, bf16[512,256]{1,0:T(8,128)(2,1)S(1)}, u32[]{:S(2)}, u32[]{:S(2)}) collective-permute-start(bf16[512,256]{1,0:T(8,128)(2,1)S(1)} %shard_map.103.own), channel_id=1, source_target_pairs={{0,256},{256,0},{1,257},{257,1},{2,258},{258,2},{3,259},{259,3},{4... | collective-permute-start | bytes 786440 | tf_op jit(solution)/shard_map/ppermute | solution.py:224
  34.7 3.8 %shard_map.102.spectrum = f32[512,512]{1,0:T(8,128)} custom-call(f32[32,16,256]{2,1,0:T(8,128)} %copy-done.2, bf16[1024,512]{1,0:T(8,128)(2,1)} %constant.37.clone.first, f32[32,1,256]{2,1,0:T(1,128)} %constant.38.clone.cos, f32[32,1,256]{2,1,0:T(1,128)} %constant.39.clone.sin, bf16[512,512]{1,0:T(8,128)(2,1)} %constant.40.clone.fwd), custom_call_target="tpu_custom_call" | custom-call | flops 1000 | bytes 1000 | tf_op jit(solution)/shard_map/pallas_call | solution.py:225
  38.5 1.9 %all-to-all-done.signal = bf16[32,16,256]{2,1,0:T(8,128)(2,1)S(1)} async-done(((bf16[32,16,256]{2,1,0:T(8,128)(2,1)}), bf16[32,16,256]{2,1,0:T(8,128)(2,1)S(1)}, u32[]{:S(2)}, u32[]{:S(2)}) %all-to-all-start) | async-done | bytes 262176 | tf_op jit(solution)/shard_map/all_to_all | solution.py:219
  41.8 1.9 %shard_map.104.dep.own = bf16[2,512,256]{2,1,0:T(8,128)(2,1)} custom-call(bf16[32,16,256]{2,1,0:T(8,128)(2,1)} %copy-done.6, f32[512,512]{1,0:T(8,128)} %shard_map.102.spectrum, bf16[512,256]{1,0:T(8,128)(2,1)} %copy-done.5, bf16[512,256]{1,0:T(8,128)(2,1)} %copy-done.9), custom_call_target="tpu_custom_call" | custom-call | flops 1000 | bytes 1000 | tf_op jit(solution)/shard_map/pallas_call | solution.py:229
  43.6 1.9 %collective-permute-start.3 = (bf16[2,512,256]{2,1,0:T(8,128)(2,1)}, bf16[2,512,256]{2,1,0:T(8,128)(2,1)S(1)}, u32[]{:S(2)}, u32[]{:S(2)}) collective-permute-start(bf16[2,512,256]{2,1,0:T(8,128)(2,1)} %shard_map.104.dep.own), channel_id=1, source_target_pairs={{0,16},{16,0},{1,17},{17,1},{2,18},{18,2},{3,19},{19,3},{4,20},{20... | collective-permute-start | bytes 1572872 | tf_op jit(solution)/shard_map/ppermute | solution.py:232
  45.6 4.8 %shard_map.105.dep.refs_1_ = bf16[32,16,256]{2,1,0:T(8,128)(2,1)} custom-call(bf16[2,512,256]{2,1,0:T(8,128)(2,1)} %shard_map.104.dep.own, bf16[32,16,256]{2,1,0:T(8,128)(2,1)} %copy-done.6, f32[512,512]{1,0:T(8,128)} %shard_map.102.spectrum, bf16[1024,512]{1,0:T(8,128)(2,1)} %constant.37.clone.first, f32[32,1,256]{2,1,0:T(1,128)} %constant.38.clone.cos, ...), custom_call_target="tpu_custom_call" | custom-call | flops 1000 | bytes 1000 | tf_op jit(solution)/shard_map/pallas_call | solution.py:233
  51.2 2.3 %shard_map.106.refs_0_.w0 = bf16[2,512,512]{2,1,0:T(8,128)(2,1)} custom-call(bf16[32,16,256]{2,1,0:T(8,128)(2,1)} %shard_map.105.dep.refs_1_, bf16[2,512,256]{2,1,0:T(8,128)(2,1)} %shard_map.104.dep.own, bf16[2,512,256]{2,1,0:T(8,128)(2,1)} %copy-done.8), custom_call_target="tpu_custom_call" | custom-call | flops 1000 | bytes 1000 | tf_op jit(solution)/shard_map/pallas_call | solution.py:236
  53.5 9.0 %collective-permute-start.4 = (bf16[2,512,512]{2,1,0:T(8,128)(2,1)}, bf16[2,512,512]{2,1,0:T(8,128)(2,1)S(1)}, u32[]{:S(2)}, u32[]{:S(2)}) collective-permute-start(bf16[2,512,512]{2,1,0:T(8,128)(2,1)} %shard_map.106.refs_0_.w0), channel_id=1, source_target_pairs={{0,32},{16,240},{32,64},{48,16},{64,96},{80,48},{96,128},{112,80},... | collective-permute-start | bytes 3145736 | tf_op jit(solution)/shard_map/ppermute | solution.py:186
  62.6 1.2 copy-done
  63.8 4.4 %all-to-all-start.1 = ((bf16[32,16,256]{2,1,0:T(8,128)(2,1)}), bf16[32,16,256]{2,1,0:T(8,128)(2,1)S(1)}, u32[]{:S(2)}, u32[]{:S(2)}) async-start(bf16[32,16,256]{2,1,0:T(8,128)(2,1)} %shard_map.107), calls=%async_computation.1 | async-start | bytes 524288 | tf_op jit(solution)/shard_map/all_to_all | solution.py:241
  68.1 11.5 %collective-permute-done.4.w1_ref = bf16[2,512,512]{2,1,0:T(8,128)(2,1)S(1)} collective-permute-done((bf16[2,512,512]{2,1,0:T(8,128)(2,1)}, bf16[2,512,512]{2,1,0:T(8,128)(2,1)S(1)}, u32[]{:S(2)}, u32[]{:S(2)}) %collective-permute-start.4) | collective-permute-done | bytes 1048608 | tf_op jit(solution)/shard_map/ppermute | solution.py:186
  79.7 4.9 %collective-permute-start.5 = (bf16[2,512,512]{2,1,0:T(8,128)(2,1)S(1)}, bf16[2,512,512]{2,1,0:T(8,128)(2,1)}, u32[]{:S(2)}, u32[]{:S(2)}) collective-permute-start(bf16[2,512,512]{2,1,0:T(8,128)(2,1)S(1)} %collective-permute-done.4.w1_ref), channel_id=1, source_target_pairs={{0,32},{16,240},{32,64},{48,16},{64,96},{80,48},{96,128},{112,80},... | collective-permute-start | bytes 3145736 | tf_op jit(solution)/shard_map/ppermute | solution.py:186
  85.3 2.3 %shard_map.108 = bf16[4,256,512]{2,1,0:T(8,128)(2,1)} custom-call(bf16[32,16,256]{2,1,0:T(8,128)(2,1)} %copy-done.10, f32[512,256]{1,0:T(8,128)} %get-tuple-element.10.query), custom_call_target="tpu_custom_call" | custom-call | flops 6000000000 | bytes 1000 | tf_op jit(solution)/shard_map/pallas_call | solution.py:243
  87.6 3.5 %all-to-all-start.2 = ((bf16[4,256,512]{2,1,0:T(8,128)(2,1)}), bf16[4,256,512]{2,1,0:T(8,128)(2,1)S(1)}, u32[]{:S(2)}, u32[]{:S(2)}) async-start(bf16[4,256,512]{2,1,0:T(8,128)(2,1)} %shard_map.108), calls=%async_computation.2 | async-start | bytes 2097152 | tf_op jit(solution)/shard_map/all_to_all | solution.py:250
  91.1 5.2 %collective-permute-done.5.w2 = bf16[2,512,512]{2,1,0:T(8,128)(2,1)} collective-permute-done((bf16[2,512,512]{2,1,0:T(8,128)(2,1)S(1)}, bf16[2,512,512]{2,1,0:T(8,128)(2,1)}, u32[]{:S(2)}, u32[]{:S(2)}) %collective-permute-start.5) | collective-permute-done | bytes 1048608 | tf_op jit(solution)/shard_map/ppermute | solution.py:186
  96.3 5.3 %collective-permute-start.6 = (bf16[2,512,512]{2,1,0:T(8,128)(2,1)}, bf16[2,512,512]{2,1,0:T(8,128)(2,1)S(1)}, u32[]{:S(2)}, u32[]{:S(2)}) collective-permute-start(bf16[2,512,512]{2,1,0:T(8,128)(2,1)} %collective-permute-done.5.w2), channel_id=1, source_target_pairs={{0,32},{16,240},{32,64},{48,16},{64,96},{80,48},{96,128},{112,80},... | collective-permute-start | bytes 3145736 | tf_op jit(solution)/shard_map/ppermute | solution.py:186
  101.6 12.0 %collective-permute-done.6.w3_ref = bf16[2,512,512]{2,1,0:T(8,128)(2,1)S(1)} collective-permute-done((bf16[2,512,512]{2,1,0:T(8,128)(2,1)}, bf16[2,512,512]{2,1,0:T(8,128)(2,1)S(1)}, u32[]{:S(2)}, u32[]{:S(2)}) %collective-permute-start.6) | collective-permute-done | bytes 1048608 | tf_op jit(solution)/shard_map/ppermute | solution.py:186
  113.7 0.8 dynamic-slice_bitcast_fusion.refs_0_
  114.5 4.9 %collective-permute-start.8 = (bf16[512,512]{1,0:T(8,128)(2,1)}, bf16[512,512]{1,0:T(8,128)(2,1)}, u32[]{:S(2)}, u32[]{:S(2)}) collective-permute-start(bf16[512,512]{1,0:T(8,128)(2,1)} %dynamic-slice_bitcast_fusion.refs_0_), channel_id=1, source_target_pairs={{0,32},{16,240},{32,64},{48,16},{64,96},{80,48},{96,128},{112,80},... | collective-permute-start | bytes 1572872 | tf_op jit(solution)/shard_map/ppermute | solution.py:186
  119.4 1.9 %collective-permute-start.7 = (bf16[4,256,512]{2,1,0:T(8,128)(2,1)S(1)}, bf16[4,256,512]{2,1,0:T(8,128)(2,1)S(1)}, u32[]{:S(2)}, u32[]{:S(2)}) collective-permute-start(bf16[4,256,512]{2,1,0:T(8,128)(2,1)S(1)} %shard_map.109.g_own), channel_id=1, source_target_pairs={{0,16},{16,0},{1,17},{17,1},{2,18},{18,2},{3,19},{19,3},{4,20},{20... | collective-permute-start | bytes 3145736 | tf_op jit(solution)/shard_map/ppermute | solution.py:252
  121.4 4.4 %collective-permute-done.8.refs_1_ = bf16[512,512]{1,0:T(8,128)(2,1)} collective-permute-done((bf16[512,512]{1,0:T(8,128)(2,1)}, bf16[512,512]{1,0:T(8,128)(2,1)}, u32[]{:S(2)}, u32[]{:S(2)}) %collective-permute-start.8) | collective-permute-done | bytes 524320 | tf_op jit(solution)/shard_map/ppermute | solution.py:186
  125.8 4.9 %shard_map.111 = (bf16[4,256,512]{2,1,0:T(8,128)(2,1)S(1)}, bf16[4,256,512]{2,1,0:T(8,128)(2,1)S(1)}) custom-call(s32[3]{0:T(128)S(1)} %pad_add_fusion.place, bf16[4,256,512]{2,1,0:T(8,128)(2,1)S(1)} %shard_map.109.g_own, bf16[4,256,512]{2,1,0:T(8,128)(2,1)S(1)} %collective-permute-done.7.other_ref, bf16[2,512,512]{2,1,0:T(8,128)(2,1)S(1)} %copy-done.1, ...), custom_call_target="tpu_custom_call" | custom-call | flops 1000 | bytes 1000 | tf_op jit(solution)/shard_map/pallas_call | solution.py:254
  130.8 6.0 %collective-permute-start.9 = (bf16[4,256,512]{2,1,0:T(8,128)(2,1)S(1)}, bf16[4,256,512]{2,1,0:T(8,128)(2,1)S(1)}, u32[]{:S(2)}, u32[]{:S(2)}) collective-permute-start(bf16[4,256,512]{2,1,0:T(8,128)(2,1)S(1)} %get-tuple-element.12), channel_id=1, source_target_pairs={{0,16},{16,0},{1,17},{17,1},{2,18},{18,2},{3,19},{19,3},{4,20},{20... | collective-permute-start | bytes 3145736 | tf_op jit(solution)/shard_map/ppermute | solution.py:270
  136.8 2.3 %collective-permute-done.9 = bf16[4,256,512]{2,1,0:T(8,128)(2,1)S(1)} collective-permute-done((bf16[4,256,512]{2,1,0:T(8,128)(2,1)S(1)}, bf16[4,256,512]{2,1,0:T(8,128)(2,1)S(1)}, u32[]{:S(2)}, u32[]{:S(2)}) %collective-permute-start.9) | collective-permute-done | bytes 1048608 | tf_op jit(solution)/shard_map/ppermute | solution.py:270
  139.3 18.0 %all_to_all.20 = bf16[4,256,512]{2,1,0:T(8,128)(2,1)S(1)} all-to-all(bf16[4,256,512]{2,1,0:T(8,128)(2,1)S(1)} %add_convert_fusion), channel_id=1, replica_groups=mesh['yl'=2,'z'=8,'c'=2,'x'=4,'yh'=4] {'x'}, dimensions={0} | all-to-all | bytes 2097152 | tf_op jit(solution)/shard_map/all_to_all | solution.py:271
  157.4 0.9 reduce_sum.12
  (37 shorter events, 5.5 us)
Async XLA Ops:
  0.0 29.4 %collective-permute-start.1 = (bf16[512,256]{1,0:T(8,128)(2,1)}, bf16[512,256]{1,0:T(8,128)(2,1)S(1)}, u32[]{:S(2)}, u32[]{:S(2)}) collective-permute-start(bf16[512,256]{1,0:T(8,128)(2,1)} %param.13), channel_id=1, source_target_pairs={{0,0},{1,32},{2,64},{3,96},{32,1},{33,33},{34,65},{35,97},{64,2},{... | collective-permute-start | bytes 786440 | tf_op jit(solution)/shard_map/ppermute | solution.py:211
  2.3 31.5 %copy-start.7 = (f32[8192,16]{0,1:T(8,128)S(1)}, f32[8192,16]{0,1:T(8,128)}, u32[]{:S(2)}) copy-start(f32[8192,16]{0,1:T(8,128)} %param.12) | copy-start | bytes 1572868
  2.4 8.9 %collective-permute-start = (bf16[3,2,512]{2,1,0:T(2,128)(2,1)S(1)}, bf16[3,2,512]{2,1,0:T(2,128)(2,1)S(1)}, u32[]{:S(2)}, u32[]{:S(2)}) collective-permute-start(bf16[3,2,512]{2,1,0:T(2,128)(2,1)S(1)} %slice.3), channel_id=1, source_target_pairs={{0,16},{16,32},{32,48},{48,64},{64,80},{80,96},{96,112},{112,128},... | collective-permute-start | bytes 18440 | tf_op jit(solution)/shard_map/ppermute | solution.py:210
  11.3 0.6 copy-start.11
  14.6 25.8 %all-to-all-start = ((bf16[32,16,256]{2,1,0:T(8,128)(2,1)}), bf16[32,16,256]{2,1,0:T(8,128)(2,1)S(1)}, u32[]{:S(2)}, u32[]{:S(2)}) async-start(bf16[32,16,256]{2,1,0:T(8,128)(2,1)} %get-tuple-element.9.refs_0_), calls=%async_computation | async-start | bytes 524288 | tf_op jit(solution)/shard_map/all_to_all | solution.py:219
  29.4 1.0 copy-start.3
  30.4 3.5 %copy-start.4 = (bf16[32,16,256]{2,1,0:T(8,128)(2,1)S(1)}, bf16[32,16,256]{2,1,0:T(8,128)(2,1)}, u32[]{:S(2)}) copy-start(bf16[32,16,256]{2,1,0:T(8,128)(2,1)} %get-tuple-element.9.refs_0_) | copy-start | bytes 786436
  30.4 3.5 %copy-start.5 = (bf16[512,256]{1,0:T(8,128)(2,1)}, bf16[512,256]{1,0:T(8,128)(2,1)S(1)}, u32[]{:S(2)}) copy-start(bf16[512,256]{1,0:T(8,128)(2,1)S(1)} %shard_map.103.own) | copy-start | bytes 786436
  30.4 10.0 %collective-permute-start.2 = (bf16[512,256]{1,0:T(8,128)(2,1)S(1)}, bf16[512,256]{1,0:T(8,128)(2,1)S(1)}, u32[]{:S(2)}, u32[]{:S(2)}) collective-permute-start(bf16[512,256]{1,0:T(8,128)(2,1)S(1)} %shard_map.103.own), channel_id=1, source_target_pairs={{0,256},{256,0},{1,257},{257,1},{2,258},{258,2},{3,259},{259,3},{4... | collective-permute-start | bytes 786440 | tf_op jit(solution)/shard_map/ppermute | solution.py:224
  33.9 0.8 copy-start.2
  40.4 0.7 copy-start.6
  41.1 0.7 copy-start.9
  43.6 6.8 %collective-permute-start.3 = (bf16[2,512,256]{2,1,0:T(8,128)(2,1)}, bf16[2,512,256]{2,1,0:T(8,128)(2,1)S(1)}, u32[]{:S(2)}, u32[]{:S(2)}) collective-permute-start(bf16[2,512,256]{2,1,0:T(8,128)(2,1)} %shard_map.104.dep.own), channel_id=1, source_target_pairs={{0,16},{16,0},{1,17},{17,1},{2,18},{18,2},{3,19},{19,3},{4,20},{20... | collective-permute-start | bytes 1572872 | tf_op jit(solution)/shard_map/ppermute | solution.py:232
  50.4 0.8 copy-start.8
  53.5 26.2 %collective-permute-start.4 = (bf16[2,512,512]{2,1,0:T(8,128)(2,1)}, bf16[2,512,512]{2,1,0:T(8,128)(2,1)S(1)}, u32[]{:S(2)}, u32[]{:S(2)}) collective-permute-start(bf16[2,512,512]{2,1,0:T(8,128)(2,1)} %shard_map.106.refs_0_.w0), channel_id=1, source_target_pairs={{0,32},{16,240},{32,64},{48,16},{64,96},{80,48},{96,128},{112,80},... | collective-permute-start | bytes 3145736 | tf_op jit(solution)/shard_map/ppermute | solution.py:186
  62.5 1.2 copy-start
  63.8 20.8 %all-to-all-start.1 = ((bf16[32,16,256]{2,1,0:T(8,128)(2,1)}), bf16[32,16,256]{2,1,0:T(8,128)(2,1)S(1)}, u32[]{:S(2)}, u32[]{:S(2)}) async-start(bf16[32,16,256]{2,1,0:T(8,128)(2,1)} %shard_map.107), calls=%async_computation.1 | async-start | bytes 524288 | tf_op jit(solution)/shard_map/all_to_all | solution.py:241
  79.7 16.6 %collective-permute-start.5 = (bf16[2,512,512]{2,1,0:T(8,128)(2,1)S(1)}, bf16[2,512,512]{2,1,0:T(8,128)(2,1)}, u32[]{:S(2)}, u32[]{:S(2)}) collective-permute-start(bf16[2,512,512]{2,1,0:T(8,128)(2,1)S(1)} %collective-permute-done.4.w1_ref), channel_id=1, source_target_pairs={{0,32},{16,240},{32,64},{48,16},{64,96},{80,48},{96,128},{112,80},... | collective-permute-start | bytes 3145736 | tf_op jit(solution)/shard_map/ppermute | solution.py:186
  84.6 0.7 copy-start.10
  87.6 31.8 %all-to-all-start.2 = ((bf16[4,256,512]{2,1,0:T(8,128)(2,1)}), bf16[4,256,512]{2,1,0:T(8,128)(2,1)S(1)}, u32[]{:S(2)}, u32[]{:S(2)}) async-start(bf16[4,256,512]{2,1,0:T(8,128)(2,1)} %shard_map.108), calls=%async_computation.2 | async-start | bytes 2097152 | tf_op jit(solution)/shard_map/all_to_all | solution.py:250
  96.3 17.4 %collective-permute-start.6 = (bf16[2,512,512]{2,1,0:T(8,128)(2,1)}, bf16[2,512,512]{2,1,0:T(8,128)(2,1)S(1)}, u32[]{:S(2)}, u32[]{:S(2)}) collective-permute-start(bf16[2,512,512]{2,1,0:T(8,128)(2,1)} %collective-permute-done.5.w2), channel_id=1, source_target_pairs={{0,32},{16,240},{32,64},{48,16},{64,96},{80,48},{96,128},{112,80},... | collective-permute-start | bytes 3145736 | tf_op jit(solution)/shard_map/ppermute | solution.py:186
  114.5 11.3 %collective-permute-start.8 = (bf16[512,512]{1,0:T(8,128)(2,1)}, bf16[512,512]{1,0:T(8,128)(2,1)}, u32[]{:S(2)}, u32[]{:S(2)}) collective-permute-start(bf16[512,512]{1,0:T(8,128)(2,1)} %dynamic-slice_bitcast_fusion.refs_0_), channel_id=1, source_target_pairs={{0,32},{16,240},{32,64},{48,16},{64,96},{80,48},{96,128},{112,80},... | collective-permute-start | bytes 1572872 | tf_op jit(solution)/shard_map/ppermute | solution.py:186
  119.4 6.4 %collective-permute-start.7 = (bf16[4,256,512]{2,1,0:T(8,128)(2,1)S(1)}, bf16[4,256,512]{2,1,0:T(8,128)(2,1)S(1)}, u32[]{:S(2)}, u32[]{:S(2)}) collective-permute-start(bf16[4,256,512]{2,1,0:T(8,128)(2,1)S(1)} %shard_map.109.g_own), channel_id=1, source_target_pairs={{0,16},{16,0},{1,17},{17,1},{2,18},{18,2},{3,19},{19,3},{4,20},{20... | collective-permute-start | bytes 3145736 | tf_op jit(solution)/shard_map/ppermute | solution.py:252
  121.4 4.4 %copy-start.1 = (bf16[2,512,512]{2,1,0:T(8,128)(2,1)S(1)}, bf16[2,512,512]{2,1,0:T(8,128)(2,1)}, u32[]{:S(2)}) copy-start(bf16[2,512,512]{2,1,0:T(8,128)(2,1)} %shard_map.106.refs_0_.w0) | copy-start | bytes 3145732
  130.8 8.2 %collective-permute-start.9 = (bf16[4,256,512]{2,1,0:T(8,128)(2,1)S(1)}, bf16[4,256,512]{2,1,0:T(8,128)(2,1)S(1)}, u32[]{:S(2)}, u32[]{:S(2)}) collective-permute-start(bf16[4,256,512]{2,1,0:T(8,128)(2,1)S(1)} %get-tuple-element.12), channel_id=1, source_target_pairs={{0,16},{16,0},{1,17},{17,1},{2,18},{18,2},{3,19},{19,3},{4,20},{20... | collective-permute-start | bytes 3145736 | tf_op jit(solution)/shard_map/ppermute | solution.py:270
